TPU v7x, 128 devices: a whole 4x4x4 slice. The times are simulated.
128 devices in a mesh: dp: 4 (over x), seq: 32 (over y, z, core).
Axes of the slice: x: 4, y: 4, z: 4, core: 2. Of those that a mesh axis runs over, the one named last changes fastest.
Arguments:
- residual_in: bfloat16 [4, 4096, 4096], P('dp', 'seq'), may hold values from -6 to 6
- se_streams: bfloat16 [4, 4096, 12288], P('dp', 'seq'), may hold values from -6 to 6
- cotangent: bfloat16 [4, 4096, 4096], P('dp', 'seq'), may hold values from -6 to 6
- feat_short: float32 [3, 12288], replicated, may hold values from -3.5 to 3.5
- feat_medium: float32 [3, 12288], replicated, may hold values from -3.5 to 3.5
- short_filter: float32 [7, 4096], replicated, may hold values from -2 to 2
- medium_filter_weight: bfloat16 [128, 256], replicated, may hold values from -0.5 to 0.5
Outputs:
- grad_residual: bfloat16 [4, 4096, 4096], P('dp', 'seq')
- grad_streams: bfloat16 [4, 4096, 12288], P('dp', 'seq')
- grad_feat_short: float32 [3, 12288], P(None, 'seq')
- grad_feat_medium: float32 [3, 12288], P(None, 'seq')
- grad_short_filter: float32 [7, 4096], P(None, 'seq')
- grad_medium_filter: float32 [128, 256], P(None, 'seq')
All inputs are finite; a program needn't handle non-finite values.
Results may differ from a plain program's by a relative error of at most 0.011.
Values may be sent and summed in bfloat16 or wider, within the bound.
No kernel may reach another device: no remote copies, remote signals or barrier semaphores. Data moves between devices by JAX's collectives and lax.ppermute only.
A program may use at most 320 MiB of HBM per device.

v0:
```python
import math

import jax
import jax.numpy as jnp
import numpy as np
from jax import lax
from jax.sharding import PartitionSpec as P


def from_behind(array, axis, by):
    peers = lax.axis_size(axis)
    pairs = [(i, i + by) for i in range(peers) if 0 <= i + by < peers]
    return lax.ppermute(array, axis, pairs)


def causal_sum(filters, extended_rows, tok_rows):
    length = filters.shape[0]
    summed = filters[0] * extended_rows[length - 1 : length - 1 + tok_rows]
    for offset in range(1, length):
        summed = (
            summed
            + filters[offset] * extended_rows[length - 1 - offset : length - 1 - offset + tok_rows]
        )
    return summed


def ahead_sum(filters, extended_rows, tok_rows):
    summed = filters[0] * extended_rows[0:tok_rows]
    for offset in range(1, filters.shape[0]):
        summed = summed + filters[offset] * extended_rows[offset : offset + tok_rows]
    return summed


def tap_gradient(gradient_rows, history, length):
    tok_rows = gradient_rows.shape[0]
    return jnp.stack(
        [
            jnp.sum(
                gradient_rows * history[length - 1 - offset : length - 1 - offset + tok_rows],
                axis=0,
            )
            for offset in range(length)
        ]
    )


def band_matrix(filters, tok_rows, lagging):
    length, groups = filters.shape
    in_span = tok_rows + length - 1
    out_pos = np.arange(tok_rows)[:, None]
    input_position = np.arange(in_span)[None, :]
    lag_index = out_pos + length - 1 - input_position if lagging else input_position - out_pos
    inside = (lag_index >= 0) & (lag_index < length)
    clipped = np.clip(lag_index, 0, length - 1).reshape(-1)
    picked = jnp.take(filters.T, jnp.asarray(clipped, dtype=jnp.int32), axis=1).reshape(
        groups, tok_rows, in_span
    )
    return jnp.where(jnp.asarray(inside)[None], picked, jnp.zeros((), filters.dtype))


def grouped_product(toeplitz, extended_rows, groups):
    in_span, channels = extended_rows.shape
    columns = extended_rows.T.reshape(groups, channels // groups, in_span)
    result_cols = jnp.einsum("gte,gce->gct", toeplitz, columns, preferred_element_type=jnp.float32)
    return result_cols.reshape(channels, result_cols.shape[2]).T


def medium_gradient(gradient_rows, extended_rows, length, groups):
    tok_rows, channels = gradient_rows.shape
    in_span = extended_rows.shape[0]
    grad_cols = gradient_rows.T.reshape(groups, channels // groups, tok_rows)
    ext_cols = extended_rows.T.reshape(groups, channels // groups, in_span)
    cross_terms = jnp.einsum(
        "gct,gce->gte", grad_cols, ext_cols, preferred_element_type=jnp.float32
    )
    flat_terms = cross_terms.reshape(groups, tok_rows * in_span)
    flat_terms = jnp.concatenate([flat_terms, jnp.zeros((groups, tok_rows), jnp.float32)], 1)
    skewed = flat_terms.reshape(groups, tok_rows, in_span + 1)[:, :, :length]
    summed = jnp.sum(skewed, axis=1)
    return summed[:, ::-1].T


def shards(
    residual_in, se_streams, cotangent, feat_short, feat_medium, short_filter, medium_filter_weight
):
    base_rows = residual_in[0]
    streams = se_streams[0]
    tok_rows, channels = base_rows.shape
    feat_len = feat_short.shape[0]
    short_len = short_filter.shape[0]
    medium_len, groups = medium_filter_weight.shape
    medium_span = medium_len - 1
    se_rim = feat_len - 1 + short_len - 1
    behind = from_behind(streams[tok_rows - se_rim :], "seq", 1)
    streams_ext = jnp.concatenate([behind, streams], 0).astype(jnp.float32)
    featured = causal_sum(feat_short, streams_ext, tok_rows + short_len - 1)
    query_se = featured[short_len - 1 :, :channels]
    key_se = featured[:, channels : 2 * channels]
    value_se = featured[:, 2 * channels :]
    product_se = key_se * value_se
    filtered_se = causal_sum(short_filter, product_se, tok_rows)
    middle = (base_rows.astype(jnp.float32) + query_se * filtered_se).astype(jnp.bfloat16)
    history_len = medium_span + feat_len - 1
    blocks = -(-history_len // tok_rows)
    received = [from_behind(middle, "seq", hop_count) for hop_count in range(blocks, 0, -1)]
    mid_long = jnp.concatenate(received + [middle], 0)[
        (blocks + 1) * tok_rows - history_len - tok_rows :
    ].astype(jnp.float32)
    mixed = causal_sum(
        feat_medium, jnp.concatenate([mid_long, mid_long, mid_long], 1), medium_span + tok_rows
    )
    query_mr = mixed[medium_span:, :channels]
    key_mr = mixed[medium_span:, channels : 2 * channels]
    value_mr = mixed[medium_span:, 2 * channels :]
    product_ext = (mixed[:, channels : 2 * channels] * mixed[:, 2 * channels :]).astype(
        jnp.bfloat16
    )
    mid_hist = mid_long[history_len - (feat_len - 1) :]
    mid_triple = jnp.concatenate([mid_hist, mid_hist, mid_hist], 1)
    filtered_mr = grouped_product(
        band_matrix(medium_filter_weight, tok_rows, True), product_ext, groups
    )
    upstream = cotangent[0].astype(jnp.float32)
    grad_query_mr = upstream * filtered_mr
    grad_filtered_mr = (upstream * query_mr).astype(jnp.bfloat16)
    grad_filtered_next = from_behind(grad_filtered_mr[:medium_span], "seq", -1)
    grad_filtered_ext = jnp.concatenate([grad_filtered_mr, grad_filtered_next], 0)
    grad_product_mr = grouped_product(
        band_matrix(medium_filter_weight, tok_rows, False), grad_filtered_ext, groups
    )
    grad_medium = medium_gradient(grad_filtered_mr, product_ext, medium_len, groups)
    grad_mixed = jnp.concatenate(
        [grad_query_mr, grad_product_mr * value_mr, grad_product_mr * key_mr], 1
    )
    mixed_next = from_behind(grad_mixed[: feat_len - 1], "seq", -1)
    back_mixed = ahead_sum(feat_medium, jnp.concatenate([grad_mixed, mixed_next], 0), tok_rows)
    grad_middle = (
        upstream
        + back_mixed[:, :channels]
        + back_mixed[:, channels : 2 * channels]
        + back_mixed[:, 2 * channels :]
    )
    grad_feat_mr = tap_gradient(grad_mixed, mid_triple, feat_len)
    grad_query_se = grad_middle * filtered_se
    grad_filtered_se = grad_middle * query_se
    filtered_next = from_behind(grad_filtered_se[: short_len - 1], "seq", -1)
    short_product_gradient = ahead_sum(
        short_filter, jnp.concatenate([grad_filtered_se, filtered_next], 0), tok_rows
    )
    grad_short = tap_gradient(grad_filtered_se, product_se, short_len)
    grad_featured = jnp.concatenate(
        [
            grad_query_se,
            short_product_gradient * value_se[short_len - 1 :],
            short_product_gradient * key_se[short_len - 1 :],
        ],
        1,
    )
    featured_next = from_behind(grad_featured[: feat_len - 1], "seq", -1)
    grad_stream_rows = ahead_sum(
        feat_short, jnp.concatenate([grad_featured, featured_next], 0), tok_rows
    )
    grad_feat_se = tap_gradient(grad_featured, streams_ext[short_len - 1 :], feat_len)
    norm_factor = 1.0 / math.sqrt(lax.axis_size("dp") * lax.axis_size("seq") * tok_rows)
    partials = (
        grad_feat_se * norm_factor,
        grad_feat_mr * norm_factor,
        grad_short * norm_factor,
        grad_medium * norm_factor,
    )
    totals = lax.psum((partials[0], partials[1], partials[2], partials[3]), ("dp", "seq"))
    token_position = lax.axis_index("seq")
    seq_count = lax.axis_size("seq")
    shares = tuple(
        (
            lax.dynamic_slice_in_dim(
                partial_value,
                token_position * (partial_value.shape[1] // seq_count),
                partial_value.shape[1] // seq_count,
                1,
            )
            for partial_value in totals
        )
    )
    return (
        grad_middle.astype(jnp.bfloat16)[None],
        grad_stream_rows.astype(jnp.bfloat16)[None],
        shares[0],
        shares[1],
        shares[2],
        shares[3],
    )


def solution(mesh):
    placed = (P("dp", "seq", None), P("dp", "seq", None), P("dp", "seq", None), P(), P(), P(), P())
    return jax.shard_map(
        shards,
        mesh=mesh,
        in_specs=placed,
        out_specs=(
            P("dp", "seq", None),
            P("dp", "seq", None),
            P(None, "seq"),
            P(None, "seq"),
            P(None, "seq"),
            P(None, "seq"),
        ),
        check_vma=False,
    )
```

profile of v0, /device:TPU:0, one launch (start us, length us, event | category | flops | bytes accessed | tf_op | source)
XLA Modules:
  0.0 836.5 jit_solution(9736397838422384464)
XLA Ops:
  13.8 3.5 copy.35
  19.6 2.7 copy.36
  22.2 4.0 maximum_convert_fusion
  26.3 4.5 copy-done.2
  30.8 12.7 %fusion.8 = f32[134,12288]{0,1:T(8,128)S(1)} fusion(f32[136,12288]{0,1:T(8,128)S(1)} %maximum_convert_fusion, f32[12288]{0:T(1024)S(1)} %bitcast.96, f32[12288]{0:T(1024)S(1)} %bitcast.98, f32[12288]{0:T(1024)S(1)} %bitcast.94), kind=kLoop, calls=%fused_computation.16 | loop fusion | flops 8232960 | bytes 26492928 | tf_op jit(solution)/shard_map/add | solution.py:21
  44.1 4.0 copy-done.5
  48.2 9.1 %fusion.46 = (bf16[128,4096]{0,1:T(8,128)(2,1)S(1)}, f32[128,4096]{0,1:T(8,128)}) fusion(f32[134,12288]{0,1:T(8,128)S(1)} %fusion.8, bf16[1,128,4096]{1,2,0:T(8,128)(2,1)S(1)} %copy-done.16, f32[134,4096]{0,1:T(8,128)S(1)} %slice_multiply_fusion.17, f32[4096]{0:T(1024)S(1)} %bitcast.122, f32[4096]{0:T(1024)S(1)} %bitcast.124, f32[4096]{0:T(1024)S(1)} %bitcast.114, ...), kind=kLoop, calls=%fused_computation.96 | loop fusion | flops 8912896 | bytes 21086208 | tf_op jit(solution)/shard_map/convert_element_type | solution.py:102
  57.4 4.7 collective-permute-start.2
  62.1 5.3 collective-permute-start.1
  68.1 90.6 %gather_fusion = bf16[32640,256]{1,0:T(8,128)(2,1)} fusion(bf16[256,128]{0,1:T(8,128)(2,1)S(1)} %bitcast.79, s32[32768]{0:T(1024)S(1)} %pad_clamp_fusion.1), kind=kCustom, calls=%fused_computation.clone | custom fusion | bytes 33553920 | tf_op jit(solution)/shard_map/jit(_take)/gather | solution.py:55
  158.7 19.0 %reshape.83 = bf16[256,128,255]{0,2,1:T(8,128)(2,1)} reshape(bf16[256,32640]{0,1:T(8,128)(2,1)} %bitcast.83) | data formatting | bytes 33423360 | tf_op jit(solution)/shard_map/reshape | solution.py:55
  177.8 23.3 %copy.47 = bf16[256,128,255]{2,1,0:T(8,128)(2,1)} copy(bf16[256,128,255]{0,2,1:T(8,128)(2,1)} %reshape.83) | data formatting | bytes 33423360 | tf_op jit(solution)/shard_map/reshape | solution.py:55
  203.8 90.6 %gather_fusion.1 = bf16[32640,256]{1,0:T(8,128)(2,1)} fusion(bf16[256,128]{0,1:T(8,128)(2,1)S(1)} %bitcast.80, s32[32768]{0:T(1024)S(1)} %pad_clamp_fusion), kind=kCustom, calls=%fused_computation.1.clone | custom fusion | bytes 33553920 | tf_op jit(solution)/shard_map/jit(_take)/gather | solution.py:55
  294.4 19.0 %reshape.84 = bf16[256,128,255]{0,2,1:T(8,128)(2,1)} reshape(bf16[256,32640]{0,1:T(8,128)(2,1)} %bitcast.84) | data formatting | bytes 33423360 | tf_op jit(solution)/shard_map/reshape | solution.py:55
  313.5 22.9 %copy.48 = bf16[256,128,255]{2,1,0:T(8,128)(2,1)} copy(bf16[256,128,255]{0,2,1:T(8,128)(2,1)} %reshape.84) | data formatting | bytes 33423360 | tf_op jit(solution)/shard_map/reshape | solution.py:55
  336.4 2.6 fusion.25
  339.0 3.1 slice.333
  342.1 15.2 %pad_maximum_fusion = f32[257,12288]{0,1:T(8,128)S(1)} fusion(f32[257,4096]{0,1:T(8,128)S(1)} %fusion.25), kind=kLoop, calls=%fused_computation.2 | loop fusion | flops 6316032 | bytes 16842752 | tf_op jit(solution)/shard_map/concatenate | solution.py:110
  357.3 12.9 %fusion.6 = f32[255,12288]{0,1:T(8,128)S(1)} fusion(f32[257,12288]{0,1:T(8,128)S(1)} %pad_maximum_fusion, f32[12288]{0:T(1024)S(1)} %bitcast.102, f32[12288]{0:T(1024)S(1)} %bitcast.104, f32[12288]{0:T(1024)S(1)} %bitcast.100), kind=kLoop, calls=%fused_computation.11 | loop fusion | flops 15667200 | bytes 50282496 | tf_op jit(solution)/shard_map/add | solution.py:21
  370.3 4.5 copy-done.6
  376.6 12.2 %fusion.2 = f32[256,16,128]{2,1,0:T(8,128)} fusion(bf16[256,16,255]{2,1,0:T(8,128)(2,1)} %bitcast.91, bf16[256,128,255]{2,1,0:T(8,128)(2,1)} %copy.47, pred[128,255]{1,0:T(8,128)(4,1)S(1)} %copy.54), kind=kOutput, calls=%fused_computation.6 | convolution fusion | flops 275742720 | bytes 20930432 | tf_op jit(solution)/shard_map/gte,gce->gct/dot_general | solution.py:64
  388.8 5.2 convert_multiply_fusion.1
  395.3 13.1 %fusion.55 = f32[256,128,255]{2,1,0:T(8,128)} fusion(bf16[256,16,128]{2,1,0:T(8,128)(2,1)S(1)} %bitcast.90, bf16[256,16,255]{2,1,0:T(8,128)(2,1)S(1)} %bitcast.92), kind=kOutput, calls=%fused_computation.124 | convolution fusion | flops 267386880 | bytes 36560896 | tf_op jit(solution)/shard_map/gct,gce->gte/dot_general | solution.py:73
  408.4 33.4 %reshape.59 = f32[256,32640]{1,0:T(8,128)} reshape(f32[256,128,255]{2,1,0:T(8,128)} %fusion.55) | data formatting | bytes 66846720 | tf_op jit(solution)/shard_map/reshape | solution.py:76
  441.9 11.9 %concatenate.43 = f32[256,32768]{1,0:T(8,128)S(1)} pad(f32[256,32640]{1,0:T(8,128)} %reshape.59, f32[]{:T(128)} %constant.23.clone.1), padding=0_0x0_128 | pad | bytes 66977796 | tf_op jit(solution)/shard_map/concatenate | solution.py:77
  453.7 14.3 %copy.49 = f32[32,8,128,256]{3,2,1,0:T(8,128)} copy(f32[32,8,128,256]{3,1,2,0:T(8,128)S(1)} %bitcast.81) | data formatting | bytes 67108864
  468.1 8.4 %slice_reduce_fusion = f32[256,128]{1,0:T(8,128)S(1)} fusion(f32[256,128,256]{2,1,0:T(8,128)} %bitcast.82), kind=kLoop, calls=%fused_computation.3 | loop fusion | flops 4161536 | bytes 16908288 | tf_op jit(solution)/shard_map/reduce_sum | solution.py:79
  476.6 12.1 %pad_maximum_fusion.3 = f32[130,12288]{0,1:T(8,128)} fusion(f32[130,4096]{0,1:T(8,128)} %slice.333), kind=kLoop, calls=%fused_computation.22 | loop fusion | flops 3194880 | bytes 8519680 | tf_op jit(solution)/shard_map/concatenate | solution.py:119
  490.4 11.6 %fusion = f32[256,16,128]{2,1,0:T(8,128)} fusion(bf16[256,16,255]{2,1,0:T(8,128)(2,1)S(1)} %bitcast.93, bf16[256,128,255]{2,1,0:T(8,128)(2,1)} %copy.48, pred[128,255]{1,0:T(8,128)(4,1)S(1)} %copy.54), kind=kOutput, calls=%fused_computation.4 | convolution fusion | flops 275742720 | bytes 20930432 | tf_op jit(solution)/shard_map/gte,gce->gct/dot_general | solution.py:64
  501.9 5.3 slice_multiply_fusion.21
  507.3 7.2 pad_maximum_fusion.4
  514.5 4.4 copy.39
  522.8 4.4 copy.40
  527.1 7.3 pad_maximum_fusion.1
  534.5 21.9 %fusion.14 = (f32[12288]{0:T(1024)S(1)}, f32[12288]{0:T(1024)S(1)}, f32[12288]{0:T(1024)S(1)}, f32[128,12288]{0,1:T(8,128)}) fusion(f32[130,12288]{0,1:T(8,128)} %pad_maximum_fusion.3, f32[128,4096]{0,1:T(8,128)S(1)} %copy-done.8, f32[128,4096]{0,1:T(8,128)S(1)} %get-tuple-element.42, f32[128,4096]{0,1:T(8,128)} %get-tuple-element.48, ...), kind=kLoop, calls=%fused_computation.40 | loop fusion | flops 20410368 | bytes 44335104 | tf_op jit(solution)/shard_map/reduce_sum | solution.py:38
  556.4 11.4 %multiply_reduce_fusion = (f32[4096]{0:T(1024)S(1)}, f32[4096]{0:T(1024)S(1)}, f32[4096]{0:T(1024)S(1)}, f32[4096]{0:T(1024)S(1)}, f32[4096]{0:T(1024)S(1)}, /*i...) fusion(f32[134,4096]{0,1:T(8,128)S(1)} %copy-done.4, ...), kind=kLoop, calls=%fused_computation.97 | loop fusion | flops 9932800 | bytes 28426240 | tf_op jit(solution)/shard_map/reduce_sum | solution.py:38
  571.2 4.2 fusion.51
  575.7 2.9 copy.42
  578.6 19.4 %slice_multiply_fusion.19 = (f32[128,4096]{0,1:T(8,128)S(1)}, f32[128,4096]{0,1:T(8,128)S(1)}) fusion(f32[134,12288]{0,1:T(8,128)} %copy-done.5, f32[6,4096]{0,1:T(8,128)} %copy.42, f32[128,4096]{0,1:T(8,128)} %copy-done.12, f32[4096]{0:T(1024)S(1)} %bitcast.123, f32[4096]{0:T(1024)S(1)} %bitcast.125, f32[4096]{0:T(1024)S(1)} %bitcast.115, ...), kind=kLoop, calls=%fused_computation.89 | loop fusion | flops 10485760 | bytes 8601600 | tf_op jit(solution)/shard_map/mul | solution.py:154
  598.0 3.6 slice_multiply_fusion.18
  601.6 7.3 pad_maximum_fusion.5
  608.8 4.4 copy.43
  615.2 4.6 collective-permute-done.6
  619.8 4.0 copy.44
  623.8 11.4 %pad_maximum_fusion.2 = f32[130,12288]{0,1:T(8,128)} fusion(f32[2,12288]{0,1:T(8,128)} %copy.44, f32[128,4096]{0,1:T(8,128)} %copy-done.9, f32[128,4096]{0,1:T(8,128)} %copy-done.11, f32[128,4096]{0,1:T(8,128)S(1)} %get-tuple-element.46), kind=kLoop, calls=%fused_computation.21 | loop fusion | flops 4792320 | bytes 12779520 | tf_op jit(solution)/shard_map/concatenate | solution.py:161
  635.2 35.2 %fusion.17 = (f32[12288]{0:T(1024)S(1)}, f32[12288]{0:T(1024)S(1)}, f32[12288]{0:T(1024)S(1)}, bf16[1,128,12288]{1,2,0:T(8,128)(2,1)}) fusion(f32[136,12288]{0,1:T(8,128)} %copy-done.2, f32[128,4096]{0,1:T(8,128)} %copy-done.9, f32[128,4096]{0,1:T(8,128)} %copy-done.11, f32[128,4096]{0,1:T(8,128)S(1)} %get-tuple-element.46, ...), kind=kLoop, calls=%fused_computation.46 | loop fusion | flops 21983232 | bytes 41189376 | tf_op jit(solution)/shard_map/reduce_sum | solution.py:38
  673.7 2.8 copy.46
  676.5 149.2 %all-reduce.4.cloned.1.call-done = (f32[3,12288]{1,0:T(4,128)}, f32[3,12288]{1,0:T(4,128)}, f32[7,4096]{1,0:T(8,128)}, f32[128,256]{0,1:T(8,128)}) async-done(((f32[3,12288]{1,0:T(4,128)}, f32[3,12288]{1,0:T(4,128)}, f32[7,4096]{1,0:T(8,128)}, f32[128,256]{0,1:T(8,128)}), (f32[3,12288]{1,0:T(4,128)}, f32[3,12288]{1,0:T(4,128)}, f32[7,4096]{1,0:T(8,128)}, f32[128,256]{0,1:T(8,128)})) %all-reduce.4.cloned.1.call-update) | async-done | bytes 540688 | tf_op jit(solution)/shard_map/psum | solution.py:171
  (117 shorter events, 34.5 us)
Async XLA Ops:
  7.2 60.9 %copy-start = (bf16[128,256]{1,0:T(8,128)(2,1)S(1)}, bf16[128,256]{1,0:T(8,128)(2,1)}, u32[]{:S(2)}) copy-start(bf16[128,256]{1,0:T(8,128)(2,1)} %param.19) | copy-start | bytes 196612
  7.2 818.5 %all-reduce.4.cloned.1.call-start = ((), (), s32[]{:S(2)}) async-start(), calls=%async_computation | async-start | bytes 1310720 | tf_op jit(solution)/shard_map/psum | solution.py:171
  8.8 10.7 %collective-permute-start = (bf16[8,12288]{1,0:T(8,128)(2,1)}, bf16[8,12288]{1,0:T(8,128)(2,1)S(1)}, u32[]{:S(2)}, u32[]{:S(2)}) collective-permute-start(bf16[8,12288]{1,0:T(8,128)(2,1)} %slice_bitcast_fusion), channel_id=1, source_target_pairs={{0,1},{1,2},{2,3},{3,4},{4,5},{5,6},{6,7},{7,8},{8,9},{9,10},{10,1... | collective-permute-start | bytes 589832 | tf_op jit(solution)/shard_map/ppermute | solution.py:13
  11.4 14.9 %copy-start.17 = (f32[1,12288]{1,0:T(1,128)}, f32[1,12288]{1,0:T(1,128)S(1)}, u32[]{:S(2)}) copy-start(f32[1,12288]{1,0:T(1,128)S(1)} %get-tuple-element.53) | copy-start | bytes 147460
  11.4 14.9 %copy-start.19 = (f32[1,12288]{1,0:T(1,128)}, f32[1,12288]{1,0:T(1,128)S(1)}, u32[]{:S(2)}) copy-start(f32[1,12288]{1,0:T(1,128)S(1)} %get-tuple-element.54) | copy-start | bytes 147460
  11.4 14.9 %copy-start.21 = (f32[1,12288]{1,0:T(1,128)}, f32[1,12288]{1,0:T(1,128)S(1)}, u32[]{:S(2)}) copy-start(f32[1,12288]{1,0:T(1,128)S(1)} %get-tuple-element.55) | copy-start | bytes 147460
  26.3 4.5 copy-start.2
  43.5 4.7 copy-start.5
  43.5 4.7 copy-start.16
  43.5 4.7 copy-start.25
  43.5 4.7 copy-start.27
  43.5 4.6 copy-start.29
  43.5 4.6 copy-start.31
  43.5 4.6 copy-start.33
  43.5 4.6 copy-start.35
  43.5 4.6 copy-start.37
  44.1 13.2 %copy-start.3 = (f32[134,4096]{0,1:T(8,128)}, f32[134,4096]{0,1:T(8,128)S(1)}, u32[]{:S(2)}) copy-start(f32[134,4096]{0,1:T(8,128)S(1)} %slice_multiply_fusion.17) | copy-start | bytes 6586372
  48.2 19.1 %copy-start.40 = (f32[3,12288]{1,0:T(4,128)S(1)}, f32[3,12288]{1,0:T(4,128)}, u32[]{:S(2)}) copy-start(f32[3,12288]{1,0:T(4,128)} %param.17) | copy-start | bytes 442372
  48.2 19.9 %copy-start.39 = (s32[32640]{0:T(1024)S(1)}, s32[32640]{0:T(1024)}, u32[]{:S(2)}) copy-start(s32[32640]{0:T(1024)} %constant.69) | copy-start | bytes 391684
  57.4 279.0 %collective-permute-start.2 = (bf16[128,4096]{0,1:T(8,128)(2,1)S(1)}, bf16[128,4096]{0,1:T(8,128)(2,1)S(1)}, u32[]{:S(2)}, u32[]{:S(2)}) collective-permute-start(bf16[128,4096]{0,1:T(8,128)(2,1)S(1)} %get-tuple-element.40), channel_id=1, source_target_pairs={{0,1},{1,2},{2,3},{3,4},{4,5},{5,6},{6,7},{7,8},{8,9},{9,10},{10,1... | collective-permute-start | bytes 3145736 | tf_op jit(solution)/shard_map/ppermute | solution.py:13
  62.1 274.3 %collective-permute-start.1 = (bf16[128,4096]{0,1:T(8,128)(2,1)S(1)}, bf16[128,4096]{0,1:T(8,128)(2,1)}, u32[]{:S(2)}, u32[]{:S(2)}) collective-permute-start(bf16[128,4096]{0,1:T(8,128)(2,1)S(1)} %get-tuple-element.40), channel_id=1, source_target_pairs={{0,2},{1,3},{2,4},{3,5},{4,6},{5,7},{6,8},{7,9},{8,10},{9,11},{10,... | collective-permute-start | bytes 3145736 | tf_op jit(solution)/shard_map/ppermute | solution.py:13
  177.8 23.3 %copy-start.41 = (pred[128,255]{1,0:T(32,128)(4,1)S(1)}, pred[128,255]{1,0:T(32,128)(4,1)}, u32[]{:S(2)}) copy-start(pred[128,255]{1,0:T(32,128)(4,1)} %constant.18.clone) | copy-start | bytes 97924
  202.7 186.1 %copy-start.14 = (bf16[1,128,4096]{1,2,0:T(8,128)(2,1)}, bf16[1,128,4096]{1,2,0:T(8,128)(2,1)S(1)}, u32[]{:S(2)}) copy-start(bf16[1,128,4096]{1,2,0:T(8,128)(2,1)S(1)} %copy.33) | copy-start | bytes 3145732
  342.1 15.2 %copy-start.23 = (f32[1,12288]{1,0:T(1,128)S(1)}, f32[1,12288]{1,0:T(1,128)}, u32[]{:S(2)}) copy-start(f32[1,12288]{1,0:T(1,128)} %get-tuple-element.51) | copy-start | bytes 147460
  342.1 15.2 %copy-start.24 = (f32[1,12288]{1,0:T(1,128)S(1)}, f32[1,12288]{1,0:T(1,128)}, u32[]{:S(2)}) copy-start(f32[1,12288]{1,0:T(1,128)} %get-tuple-element.52) | copy-start | bytes 147460
  370.3 4.5 copy-start.6
  388.8 6.5 copy-start.15
  394.0 94.7 %collective-permute-start.3 = (bf16[127,4096]{0,1:T(8,128)(2,1)S(1)}, bf16[127,4096]{0,1:T(8,128)(2,1)}, u32[]{:S(2)}, u32[]{:S(2)}) collective-permute-start(bf16[127,4096]{0,1:T(8,128)(2,1)S(1)} %bitcast.89), channel_id=1, source_target_pairs={{1,0},{2,1},{3,2},{4,3},{5,4},{6,5},{7,6},{8,7},{9,8},{10,9},{11,1... | collective-permute-start | bytes 3121160 | tf_op jit(solution)/shard_map/ppermute | solution.py:13
  501.9 5.4 copy-start.10
  507.3 7.3 copy-start.7
  519.0 3.8 collective-permute-start.4
  527.1 7.3 copy-start.8
  534.5 21.9 %copy-start.4 = (f32[134,4096]{0,1:T(8,128)S(1)}, f32[134,4096]{0,1:T(8,128)}, u32[]{:S(2)}) copy-start(f32[134,4096]{0,1:T(8,128)} %copy-done.3) | copy-start | bytes 6586372
  569.1 6.6 collective-permute-start.5
  571.2 7.3 copy-start.26
  571.2 7.3 copy-start.28
  571.2 7.3 copy-start.30
  571.2 7.3 copy-start.32
  571.2 7.3 copy-start.34
  571.2 7.3 copy-start.36
  571.2 7.3 copy-start.38
  598.0 10.8 %copy-start.11 = (f32[128,4096]{0,1:T(8,128)}, f32[128,4096]{0,1:T(8,128)S(1)}, u32[]{:S(2)}) copy-start(f32[128,4096]{0,1:T(8,128)S(1)} %get-tuple-element.38) | copy-start | bytes 6291460
  601.5 7.3 copy-start.9
  613.2 6.6 collective-permute-start.6
  623.8 11.4 %copy-start.18 = (f32[1,12288]{1,0:T(1,128)S(1)}, f32[1,12288]{1,0:T(1,128)}, u32[]{:S(2)}) copy-start(f32[1,12288]{1,0:T(1,128)} %copy-done.17) | copy-start | bytes 147460
  623.8 11.4 %copy-start.20 = (f32[1,12288]{1,0:T(1,128)S(1)}, f32[1,12288]{1,0:T(1,128)}, u32[]{:S(2)}) copy-start(f32[1,12288]{1,0:T(1,128)} %copy-done.19) | copy-start | bytes 147460
  623.8 11.4 %copy-start.22 = (f32[1,12288]{1,0:T(1,128)S(1)}, f32[1,12288]{1,0:T(1,128)}, u32[]{:S(2)}) copy-start(f32[1,12288]{1,0:T(1,128)} %copy-done.21) | copy-start | bytes 147460
  671.3 158.2 %copy-start.1 = (bf16[128,256]{1,0:T(8,128)(2,1)S(1)}, bf16[128,256]{1,0:T(8,128)(2,1)}, u32[]{:S(2)}) copy-start(bf16[128,256]{1,0:T(8,128)(2,1)} %param.19) | copy-start | bytes 196612
  (2 other events, 6.7 us)
Sparse Core Ops, SparseCore 0:
  671.4 154.2 all-reduce.3
where the time goes:
time: 845 us; the launch traced here: 837 us
  local copies, waits for them, and re-layouts  388 us (46%)
  other arithmetic  225 us (27%)
  waiting for transfers between devices  156 us (18%)
  matrix products  36.9 us (4%)
  starting transfers between devices  16.4 us (2%)
  between operations  14.8 us (2%)
    gather x2, local copies, waits for them, and re-layouts, band_matrix(): jnp.take(filters.T, jnp.asarray(clipped, dtype=jnp.int32), axis=1)  181 us
    psum x1, waiting for transfers between devices, shards(): lax.psum((partials[0], partials[1], partials[2], partials[3]), ('dp', 'se...  149 us
    reshape x4, local copies, waits for them, and re-layouts, band_matrix(): jnp.take(filters.T, jnp.asarray(clipped, dtype=jnp.int32), axis=1)  84.3 us
    reduce_sum x3, other arithmetic, tap_gradient(): jnp.sum(gradient_rows * history[length - 1 - offset:length - 1 - offset +...  68.5 us
    unnamed x91, local copies, waits for them, and re-layouts  40 us
    reshape x1, local copies, waits for them, and re-layouts, medium_gradient(): flat_terms = cross_terms.reshape(groups, tok_rows * in_span)  33.4 us
    add x2, other arithmetic, causal_sum(): summed + filters[offset] * extended_rows[length - 1 - offset:length - 1 -...  25.6 us
    dot_general x2, matrix products, grouped_product(): jnp.einsum('gte,gce->gct', toeplitz, columns, preferred_element_type=jnp....  23.7 us
  transfers between devices with their start and end apart: 8, of which 3 were waited for; matrix products, arithmetic and copies ran while one was open for 46% of the time, Pallas kernels for 0%

commit v1 on v0

v1 whole, which is shorter than its diff:
```python
import functools
import math

import jax
import jax.numpy as jnp
from jax import lax
from jax.experimental import pallas as pl
from jax.experimental.pallas import tpu as pltpu
from jax.sharding import PartitionSpec as P

F32 = jnp.float32
BF16 = jnp.bfloat16
LANES = 128
GROUP = 16
BLOCKS = LANES // GROUP
EDGE = 10
FRAME = 24
TILES = 4


def shift_rows(array, axis, by):
    peers = lax.axis_size(axis)
    return lax.ppermute(array, axis, [(i, i + by) for i in range(peers) if 0 <= i + by < peers])


def lane_blocks(shape):
    return lax.broadcasted_iota(jnp.int32, shape, 1) // GROUP


def swap_blocks(parts):
    parts = list(parts)
    block = lane_blocks(parts[0].shape)
    step = BLOCKS // 2
    while step:
        low = (block & step) == 0
        shift = GROUP * step
        for i in range(BLOCKS):
            if i & step == 0:
                first, second = parts[i], parts[i + step]
                parts[i] = jnp.where(low, first, pltpu.roll(second, shift, 1))
                parts[i + step] = jnp.where(low, pltpu.roll(first, LANES - shift, 1), second)
        step //= 2
    return parts


def taps_of(ref, lanes):
    return [ref[i : i + 1, lanes] for i in range(ref.shape[0])]


def back_taps(taps, ref, start, rows):
    total = taps[0] * ref[start : start + rows, :]
    for i in range(1, len(taps)):
        total = total + taps[i] * ref[start - i : start - i + rows, :]
    return total


def ahead_taps(taps, ref, start, rows):
    total = taps[0] * ref[start : start + rows, :]
    for i in range(1, len(taps)):
        total = total + taps[i] * ref[start + i : start + i + rows, :]
    return total


def first_kernel(rows, *refs):
    (q, k, v, res, g, pq, pk, pv, pr, nq, nk, nv, nr, ng) = refs[:14]
    (fsq, fsk, fsv, short, fmq, fmk, fmv) = refs[14:21]
    (w_own, w_edge, d_own, mid_out, q1_out, s1_out, k1_out, v1_out) = refs[21:29]
    (sq, sk, sv, sr, sg, sw, sm) = refs[29:]
    total = rows + GROUP

    @pl.when(pl.program_id(0) == 0)
    def _():
        for ref in (sq, sk, sv, sr, sg):
            ref[...] = jnp.zeros(ref.shape, F32)

    def one_tile(i, carry):
        lanes = pl.ds(pl.multiple_of(i * LANES, LANES), LANES)
        for scratch, own, before, after in (
            (sq, q, pq, nq),
            (sk, k, pk, nk),
            (sv, v, pv, nv),
            (sr, res, pr, nr),
            (sg, g, None, ng),
        ):
            if before is not None:
                scratch[FRAME - EDGE : FRAME, :] = before[:, lanes].astype(F32)
            for r in range(0, rows, GROUP):
                scratch[FRAME + r : FRAME + r + GROUP, :] = own[r : r + GROUP, lanes].astype(F32)
            scratch[FRAME + rows : FRAME + rows + EDGE, :] = after[:, lanes].astype(F32)
        tq, tk, tv = taps_of(fsq, lanes), taps_of(fsk, lanes), taps_of(fsv, lanes)
        for t in range(-GROUP, total, GROUP):
            at = FRAME + t
            k1 = back_taps(tk, sk, at, GROUP)
            v1 = back_taps(tv, sv, at, GROUP)
            sw[at : at + GROUP, :] = k1 * v1
            k1_out[i, t + GROUP : t + 2 * GROUP, :] = k1.astype(BF16)
            v1_out[i, t + GROUP : t + 2 * GROUP, :] = v1.astype(BF16)
        ts = taps_of(short, lanes)
        for t in range(-GROUP, total, GROUP):
            at = FRAME + t
            q1 = back_taps(tq, sq, at, GROUP)
            s1 = back_taps(ts, sw, at, GROUP)
            mid = (sr[at : at + GROUP, :] + q1 * s1).astype(BF16)
            sm[at : at + GROUP, :] = mid.astype(F32)
            mid_out[i, t + GROUP : t + 2 * GROUP, :] = mid
            if t >= 0:
                q1_out[i, t : t + GROUP, :] = q1.astype(BF16)
                s1_out[i, t : t + GROUP, :] = s1.astype(BF16)
        mq, mk, mv = taps_of(fmq, lanes), taps_of(fmk, lanes), taps_of(fmv, lanes)
        products, slopes = [], []
        for t in range(0, total, GROUP):
            at = FRAME + t
            m = [sm[at - j : at - j + GROUP, :] for j in range(3)]
            q2, k2, v2 = [
                taps[0] * m[0] + taps[1] * m[1] + taps[2] * m[2] for taps in (mq, mk, mv)
            ]
            products.append((k2 * v2).astype(BF16))
            slopes.append((sg[at : at + GROUP, :] * q2).astype(BF16))
        for j, part in enumerate(swap_blocks(products[:BLOCKS])):
            w_own[i, j * GROUP : (j + 1) * GROUP, :] = part
        w_edge[i] = products[BLOCKS]
        for j, part in enumerate(swap_blocks(slopes[:BLOCKS])):
            d_own[i, j * GROUP : (j + 1) * GROUP, :] = part
        d_own[i, rows : rows + GROUP, :] = slopes[BLOCKS]
        return carry

    lax.fori_loop(0, TILES, one_tile, 0)


def windows(low, high, last, block):
    rows = []
    for k in range(BLOCKS + 1):
        if k == 0:
            first, second = low, high
        elif k == BLOCKS:
            first, second = high, last
        else:
            shift = LANES - GROUP * k
            second = pltpu.roll(high, shift, 1)
            first = jnp.where(block < BLOCKS - k, pltpu.roll(low, shift, 1), second)
        rows.append(jnp.concatenate([first, second], 1))
    return jnp.concatenate(rows, 0)


def second_kernel(rows, channels, *refs):
    (q, k, v, g, pq, pk, pv, ng) = refs[:8]
    (w_own, w_edge, w_prev, d_own, d_next, taps_fwd, taps_rev) = refs[8:15]
    (mid_in, q1_in, s1_in, k1_in, v1_in) = refs[15:20]
    (fsq, fsk, fsv, short, fmq, fmk, fmv) = refs[20:27]
    (grad_res, grad_streams, sums) = refs[27:30]
    (sq, sk, sv, sg, sm, sw, dq, dk, dv, d1, eq, ek, ev, out_buf, sems) = refs[30:]
    step = pl.program_id(0)
    steps = pl.num_programs(0)
    slot = lax.rem(step, 2)
    width = TILES * LANES
    base = GROUP

    def copies(at_step, at_slot):
        return [
            pltpu.make_async_copy(
                out_buf.at[at_slot, x],
                grad_streams.at[
                    :, pl.ds(pl.multiple_of(x * channels + at_step * width, width), width)
                ],
                sems.at[at_slot, x],
            )
            for x in range(3)
        ]

    @pl.when(step == 0)
    def _():
        for ref in (sg, dq, dk, dv, d1, eq, ek, ev):
            ref[...] = jnp.zeros(ref.shape, F32)

    @pl.when(step >= 2)
    def _():
        for copy in copies(step - 2, slot):
            copy.wait()

    iota_row = lax.broadcasted_iota(jnp.int32, (GROUP, LANES), 0)
    iota_lane = lax.broadcasted_iota(jnp.int32, (GROUP, LANES), 1)

    def one_tile(i, carry):
        lanes = pl.ds(pl.multiple_of(i * LANES, LANES), LANES)
        tile = step * TILES + i
        block = lane_blocks((GROUP, LANES))
        s2_parts, w2_parts = [], []
        s2_last = jnp.zeros((GROUP, LANES), BF16)
        w2_last = jnp.zeros((GROUP, LANES), BF16)
        edge_w = w_edge[i]
        edge_d = d_next[i, rows : rows + GROUP, :]
        for j in range(BLOCKS):
            part = slice(j * GROUP, (j + 1) * GROUP)
            fwd = jnp.broadcast_to(taps_fwd[pl.ds(i * BLOCKS + j, 1), :], (GROUP, LANES))
            rev = jnp.broadcast_to(taps_rev[pl.ds(i * BLOCKS + j, 1), :], (GROUP, LANES))
            fwd = pltpu.roll(fwd, 0, 1, stride=1, stride_axis=0)
            rev = pltpu.roll(rev, 1, 1, stride=1, stride_axis=0)
            ahead = jnp.concatenate(
                [
                    jnp.where(iota_lane >= iota_row, fwd, 0.0),
                    jnp.where(iota_lane < iota_row, fwd, 0.0)[:, :GROUP],
                ],
                1,
            ).astype(BF16)
            lag = jnp.concatenate(
                [
                    jnp.where(iota_lane > iota_row, rev, 0.0),
                    jnp.where(iota_lane <= iota_row, rev, 0.0)[:, :GROUP],
                ],
                1,
            ).astype(BF16)
            turn = (LANES - GROUP * j) % LANES
            own_d = d_own[i, part, :]
            win = windows(
                w_prev[i, part, :],
                w_own[i, part, :],
                pltpu.roll(edge_w, turn, 1) if turn else edge_w,
                block,
            )
            s2 = jnp.dot(lag, win, preferred_element_type=F32).astype(BF16)
            cross = lax.dot_general(
                own_d, win[:, :LANES], (((1,), (1,)), ((), ())), preferred_element_type=F32
            )
            win = windows(
                own_d,
                d_next[i, part, :],
                pltpu.roll(edge_d, turn, 1) if turn else edge_d,
                block,
            )
            w2 = jnp.dot(ahead, win, preferred_element_type=F32).astype(BF16)
            s2_parts.append(s2[:, :LANES])
            w2_parts.append(w2[:, :LANES])
            here = block == j
            s2_end, w2_end = s2[:, LANES:], w2[:, LANES:]
            if j:
                s2_end, w2_end = (
                    pltpu.roll(s2_end, GROUP * j, 1),
                    pltpu.roll(w2_end, GROUP * j, 1),
                )
            s2_last = jnp.where(here, s2_end, s2_last)
            w2_last = jnp.where(here, w2_end, w2_last)
            spread = jnp.concatenate(
                [cross[:, LANES:], jnp.zeros((GROUP, LANES - GROUP), F32)], 1
            )
            spread = jnp.where(iota_lane <= iota_row, spread, cross[:, :LANES])
            spread = pltpu.roll(spread, LANES - 1, 1)
            fold = GROUP // 2
            spread = spread[:fold] + pltpu.roll(spread[fold:], LANES - fold, 1)
            while fold > 1:
                fold //= 2
                spread = spread + pltpu.roll(pltpu.roll(spread, 8 - fold, 0), LANES - fold, 1)
            sums[pl.ds(tile, 1), 25 + j : 26 + j, :] = spread[:1][None]
        s2_parts = swap_blocks(s2_parts) + [s2_last]
        w2_parts = swap_blocks(w2_parts) + [w2_last]

        for r in range(0, rows + 2 * GROUP, GROUP):
            sm[r : r + GROUP, :] = mid_in[i, r : r + GROUP, :].astype(F32)
        for r in range(0, rows + GROUP, GROUP):
            sw[r : r + GROUP, :] = k1_in[i, r : r + GROUP, :].astype(F32) * v1_in[
                i, r : r + GROUP, :
            ].astype(F32)
        for scratch, own, before in ((sq, q, pq), (sk, k, pk), (sv, v, pv)):
            scratch[base - EDGE : base, :] = before[:, lanes].astype(F32)
            for r in range(0, rows, GROUP):
                scratch[base + r : base + r + GROUP, :] = own[r : r + GROUP, lanes].astype(F32)
        for r in range(0, rows, GROUP):
            sg[r : r + GROUP, :] = g[r : r + GROUP, lanes].astype(F32)
        sg[rows : rows + EDGE, :] = ng[:, lanes].astype(F32)

        def put(row, x, taps, totals):
            column = x * (channels // LANES) + tile
            to = lax.div(column, 3)
            place = lax.rem(column, 3)
            for n in range(taps):
                sums[pl.ds(to, 1), pl.ds(row + 3 * n + place, 1), :] = jnp.sum(
                    totals[n], axis=0, keepdims=True
                )[None]

        mk, mv = taps_of(fmk, lanes), taps_of(fmv, lanes)
        acc = [[jnp.zeros((GROUP, LANES), F32) for _ in range(3)] for _ in range(3)]
        for a in range(BLOCKS + 1):
            t = a * GROUP
            m = [sm[base + t - j : base + t - j + GROUP, :] for j in range(3)]
            k2 = mk[0] * m[0] + mk[1] * m[1] + mk[2] * m[2]
            v2 = mv[0] * m[0] + mv[1] * m[1] + mv[2] * m[2]
            s2 = s2_parts[a].astype(F32)
            w2 = w2_parts[a].astype(F32)
            parts = (sg[t : t + GROUP, :] * s2, w2 * v2, w2 * k2)
            for x, (ref, value) in enumerate(zip((dq, dk, dv), parts)):
                ref[t : t + GROUP, :] = value
                if a < BLOCKS:
                    for j in range(3):
                        acc[x][j] = acc[x][j] + value * m[j]
        for x in range(3):
            put(9, x, 3, acc[x])
        mq = taps_of(fmq, lanes)
        for a in range(BLOCKS + 1):
            t = a * GROUP
            dmid = (
                sg[t : t + GROUP, :]
                + ahead_taps(mq, dq, t, GROUP)
                + ahead_taps(mk, dk, t, GROUP)
                + ahead_taps(mv, dv, t, GROUP)
            )
            if a < BLOCKS:
                grad_res[t : t + GROUP, lanes] = dmid.astype(BF16)
            d1[t : t + GROUP, :] = dmid * q1_in[i, t : t + GROUP, :].astype(F32)
            eq[t : t + GROUP, :] = dmid * s1_in[i, t : t + GROUP, :].astype(F32)
        ts = taps_of(short, lanes)
        acc = [jnp.zeros((GROUP, LANES), F32) for _ in range(len(ts))]
        for a in range(BLOCKS + 1):
            t = a * GROUP
            dw1 = ahead_taps(ts, d1, t, GROUP)
            ek[t : t + GROUP, :] = dw1 * v1_in[i, base + t : base + t + GROUP, :].astype(F32)
            ev[t : t + GROUP, :] = dw1 * k1_in[i, base + t : base + t + GROUP, :].astype(F32)
            if a < BLOCKS:
                slope = d1[t : t + GROUP, :]
                for n in range(len(ts)):
                    acc[n] = acc[n] + slope * sw[base + t - n : base + t - n + GROUP, :]
        for n in range(len(ts)):
            sums[pl.ds(tile, 1), 18 + n : 19 + n, :] = jnp.sum(acc[n], axis=0, keepdims=True)[None]
        for x, (ref, taps_ref, stream) in enumerate(((eq, fsq, sq), (ek, fsk, sk), (ev, fsv, sv))):
            taps = taps_of(taps_ref, lanes)
            acc = [jnp.zeros((GROUP, LANES), F32) for _ in range(3)]
            for a in range(BLOCKS):
                t = a * GROUP
                e = [ref[t + j : t + j + GROUP, :] for j in range(3)]
                out_buf[slot, x, t : t + GROUP, lanes] = (
                    taps[0] * e[0] + taps[1] * e[1] + taps[2] * e[2]
                ).astype(BF16)
                for j in range(3):
                    acc[j] = acc[j] + e[0] * stream[base + t - j : base + t - j + GROUP, :]
            put(0, x, 3, acc)
        return carry

    lax.fori_loop(0, TILES, one_tile, 0)
    for copy in copies(step, slot):
        copy.start()

    @pl.when(step == steps - 1)
    def _():
        @pl.when(steps > 1)
        def _():
            for copy in copies(step - 1, 1 - slot):
                copy.wait()

        for copy in copies(step, slot):
            copy.wait()


def columns(rows, first=0):
    width = TILES * LANES
    return pl.BlockSpec((rows, width), lambda j: (0, first + j))


def tiled(rows):
    return pl.BlockSpec((TILES, rows, LANES), lambda j: (j, 0, 0))


def shards(
    residual_in, se_streams, cotangent, feat_short, feat_medium, short_filter, medium_filter_weight
):
    res, streams, g = residual_in[0], se_streams[0], cotangent[0]
    rows, channels = res.shape
    seqs, slabs = lax.axis_size("seq"), lax.axis_size("dp")
    tiles = channels // LANES
    steps = tiles // TILES
    groups = medium_filter_weight.shape[1]
    before = shift_rows(
        jnp.concatenate([streams[rows - EDGE :], res[rows - EDGE :]], 1), "seq", 1
    )
    after = shift_rows(
        jnp.concatenate([streams[:EDGE], res[:EDGE], g[:EDGE]], 1), "seq", -1
    )
    edge = functools.partial(columns, EDGE)
    tap_specs = [columns(3, x * steps) for x in range(3)]
    filters = (feat_short,) * 3 + (short_filter,) + (feat_medium,) * 3
    filter_specs = tap_specs + [columns(short_filter.shape[0])] + tap_specs
    long, ext = rows + 2 * GROUP, rows + GROUP
    saved = [long, ext, ext, long, long]
    scratch = pltpu.VMEM((FRAME + ext, LANES), F32)
    w_own, w_edge, d_own, mid, q1, s1, k1, v1 = pl.pallas_call(
        functools.partial(first_kernel, rows),
        grid=(steps,),
        in_specs=[columns(rows, x * steps) for x in range(3)]
        + [columns(rows)] * 2
        + [edge(x * steps) for x in range(4)]
        + [edge(x * steps) for x in range(5)]
        + filter_specs,
        out_specs=[tiled(rows), tiled(GROUP), tiled(ext)] + [tiled(n) for n in saved],
        out_shape=[
            jax.ShapeDtypeStruct((tiles, n, LANES), BF16) for n in [rows, GROUP, ext] + saved
        ],
        scratch_shapes=[scratch] * 7,
        compiler_params=pltpu.CompilerParams(vmem_limit_bytes=48 * 1024 * 1024),
        name="products",
    )(
        *[streams] * 3, res, g, *[before] * 4, *[after] * 5, *filters
    )
    w_prev = shift_rows(w_own, "seq", 1)
    d_next = shift_rows(d_own, "seq", -1)
    taps_fwd = medium_filter_weight.T.astype(F32)
    taps_rev = taps_fwd[:, ::-1]
    per_step = pl.BlockSpec((TILES * BLOCKS, LANES), lambda j: (j, 0))
    row_buf = lambda n: pltpu.VMEM((n, LANES), F32)
    grad_res, grad_streams, sums = pl.pallas_call(
        functools.partial(second_kernel, rows, channels),
        grid=(steps,),
        in_specs=[columns(rows, x * steps) for x in range(3)]
        + [columns(rows)]
        + [edge(x * steps) for x in range(3)]
        + [edge(4 * steps)]
        + [tiled(rows), tiled(GROUP), tiled(rows), tiled(ext), tiled(ext)]
        + [per_step] * 2
        + [tiled(n) for n in saved]
        + filter_specs,
        out_specs=[
            columns(rows),
            pl.BlockSpec(memory_space=pl.ANY),
            pl.BlockSpec((tiles, 40, LANES), lambda j: (0, 0, 0)),
        ],
        out_shape=[
            jax.ShapeDtypeStruct((rows, channels), BF16),
            jax.ShapeDtypeStruct((rows, 3 * channels), BF16),
            jax.ShapeDtypeStruct((tiles, 40, LANES), F32),
        ],
        scratch_shapes=[row_buf(GROUP + rows)] * 3
        + [row_buf(ext), row_buf(long), row_buf(ext)]
        + [row_buf(ext + 8)] * 7
        + [
            pltpu.VMEM((2, 3, rows, TILES * LANES), BF16),
            pltpu.SemaphoreType.DMA((2, 3)),
        ],
        compiler_params=pltpu.CompilerParams(vmem_limit_bytes=48 * 1024 * 1024),
        name="gradients",
    )(
        *[streams] * 3, g, *[before] * 3, after,
        w_own, w_edge, w_prev, d_own, d_next, taps_fwd, taps_rev,
        mid, q1, s1, k1, v1, *filters
    )
    norm_factor = 1.0 / math.sqrt(slabs * seqs * rows)
    parts = lax.all_to_all(sums[:, :33], "seq", split_axis=0, concat_axis=0, tiled=True)
    share = jnp.sum(parts, axis=0) * norm_factor
    others = [
        lax.ppermute(share, "dp", [(i, (i + n) % slabs) for i in range(slabs)])
        for n in range(1, slabs)
    ]
    for other in others:
        share = share + other
    return (
        grad_res[None],
        grad_streams[None],
        share[0:9].reshape(3, -1),
        share[9:18].reshape(3, -1),
        share[18:25],
        share[25:33, ::-1].T,
    )


def solution(mesh):
    placed = (P("dp", "seq", None), P("dp", "seq", None), P("dp", "seq", None), P(), P(), P(), P())
    return jax.shard_map(
        shards,
        mesh=mesh,
        in_specs=placed,
        out_specs=(
            P("dp", "seq", None),
            P("dp", "seq", None),
            P(None, "seq"),
            P(None, "seq"),
            P(None, "seq"),
            P(None, "seq"),
        ),
        check_vma=False,
    )
```

time: 845 us -> 128 us (0.15)
  local copies, waits for them, and re-layouts: 388 us -> 5.25 us
  other arithmetic: 225 us -> 0.19 us
  waiting for transfers between devices: 156 us -> 6.88 us
  Pallas kernels: 0 us -> 56.3 us
  blocking collectives: 0 us -> 37.1 us
  matrix products: 36.9 us -> 0 us
  between operations: 14.8 us -> 0.78 us
    gather x2 -> x0, local copies, waits for them, and re-layouts: 181 us -> none  [band_matrix(): jnp.take(filters.T, jnp.asarray(clipped, dtype=jnp.int32), axis=1)]
    psum x1 -> x0, waiting for transfers between devices: 149 us -> none  [shards(): lax.psum((partials[0], partials[1], partials[2], partials[3]), ('dp', 'se...]
    reshape x5 -> x2, local copies, waits for them, and re-layouts: 118 us -> 1.2 us  [the longest x1 0.6 us: shards(): share[9:18].reshape(3, -1)]
    reduce_sum x4 -> x1, other arithmetic: 76.9 us -> 0.05 us  [shards(): share = jnp.sum(parts, axis=0) * norm_factor]
    concatenate x7 -> x2, other arithmetic: 62.1 us -> 0.11 us  [the longest x1 0.06 us: shards(): jnp.concatenate([streams[:EDGE], res[:EDGE], g[:EDGE]], 1)]
    pallas_call x0 -> x2, Pallas kernels: none -> 56.3 us  [the longest x1 39.8 us: shards(): pl.pallas_call(functools.partial(second_kernel, rows, channels), grid=(st...]
    mul x10 -> x1, other arithmetic: 41.2 us -> 0.01 us  [shards(): share = jnp.sum(parts, axis=0) * norm_factor]
    unnamed x91 -> x13, local copies, waits for them, and re-layouts: 40 us -> 0.3 us
  transfers between devices with their start and end apart: 8 -> 7, of which waited for: 3 -> 5; matrix products, arithmetic and copies ran while one was open for 46% -> 0% of each run, Pallas kernels for 0% -> 0%
where the time goes in v1:
time: 128 us; the launch traced here: 127 us
  Pallas kernels  56.3 us (44%)
  blocking collectives  37.1 us (29%)
  starting transfers between devices  20.8 us (16%)
  waiting for transfers between devices  6.88 us (5%)
  local copies, waits for them, and re-layouts  5.25 us (4%)
    pallas_call x1, Pallas kernels, shards(): pl.pallas_call(functools.partial(second_kernel, rows, channels), grid=(st...  39.8 us
    all_to_all x1, blocking collectives, shards(): lax.all_to_all(sums[:, :33], 'seq', split_axis=0, concat_axis=0, tiled=True)  37.1 us
    pallas_call x1, Pallas kernels, shards(): pl.pallas_call(functools.partial(first_kernel, rows), grid=(steps,), in_s...  16.5 us
    ppermute x4, starting transfers between devices, shift_rows(): lax.ppermute(array, axis, [(i, i + by) for i in range(peers) if 0 <= i +...  15.7 us
    ppermute x3, starting transfers between devices, shards(): lax.ppermute(share, 'dp', [(i, (i + n) % slabs) for i in range(slabs)])  5.13 us
    ppermute x3, waiting for transfers between devices, shards(): lax.ppermute(share, 'dp', [(i, (i + n) % slabs) for i in range(slabs)])  4.11 us
    ppermute x4, waiting for transfers between devices, shift_rows(): lax.ppermute(array, axis, [(i, i + by) for i in range(peers) if 0 <= i +...  2.77 us
  transfers between devices with their start and end apart: 7, of which 5 were waited for; matrix products, arithmetic and copies ran while one was open for 0% of the time, Pallas kernels for 0%

profile of v1, /device:TPU:0, one launch (start us, length us, event | category | flops | bytes accessed | tf_op | source)
XLA Modules:
  0.0 127.3 jit_solution(11353295266774013782)
XLA Ops:
  0.6 0.0 copy-start.2
  0.6 1.3 %slice_bitcast_fusion = (bf16[10,12288]{1,0:T(8,128)(2,1)S(1)}, bf16[10,12288]{1,0:T(8,128)(2,1)S(1)}) fusion(bf16[1,128,12288]{2,1,0:T(8,128)(2,1)} %param.8), kind=kLoop, calls=%fused_computation.2 | loop fusion | bytes 983040 | tf_op jit(solution)/shard_map/slice | solution.py:373
  1.9 0.2 copy-done.2
  2.1 1.0 slice_bitcast_fusion.3
  3.1 0.0 copy-start
  3.1 0.0 copy-start.1
  3.1 0.0 copy-start.3
  3.1 0.0 copy-start.4
  3.1 0.1 pad_maximum_fusion
  3.2 1.4 %collective-permute-start.1 = (bf16[10,20480]{1,0:T(8,128)(2,1)S(1)}, bf16[10,20480]{1,0:T(8,128)(2,1)S(1)}, u32[]{:S(2)}, u32[]{:S(2)}) collective-permute-start(bf16[10,20480]{1,0:T(8,128)(2,1)S(1)} %pad_maximum_fusion), channel_id=1, source_target_pairs={{1,0},{2,1},{3,2},{4,3},{5,4},{6,5},{7,6},{8,7},{9,8},{10,9},{11,1... | collective-permute-start | bytes 1228808 | tf_op jit(solution)/shard_map/ppermute | solution.py:23
  4.7 3.1 %collective-permute-start = (bf16[10,16384]{1,0:T(8,128)(2,1)S(1)}, bf16[10,16384]{1,0:T(8,128)(2,1)S(1)}, u32[]{:S(2)}, u32[]{:S(2)}) collective-permute-start(bf16[10,16384]{1,0:T(8,128)(2,1)S(1)} %pad_maximum_fusion.1), channel_id=1, source_target_pairs={{0,1},{1,2},{2,3},{3,4},{4,5},{5,6},{6,7},{7,8},{8,9},{9,10},{10,1... | collective-permute-start | bytes 983048 | tf_op jit(solution)/shard_map/ppermute | solution.py:23
  7.8 1.5 %collective-permute-done.refs_5_.refs_6_.refs_7_.refs_8_.refs_4_ = bf16[10,16384]{1,0:T(8,128)(2,1)S(1)} collective-permute-done((bf16[10,16384]{1,0:T(8,128)(2,1)S(1)}, bf16[10,16384]{1,0:T(8,128)(2,1)S(1)}, u32[]{:S(2)}, u32[]{:S(2)}) %collective-permute-start) | collective-permute-done | bytes 327712 | tf_op jit(solution)/shard_map/ppermute | solution.py:23
  9.3 0.0 collective-permute-done.1.refs_9_.refs_10_.refs_11_.refs_12_.refs_13_.refs_7_
  9.3 0.0 copy-done
  9.3 0.0 copy-done.1
  9.3 0.0 copy-done.3
  9.3 0.0 copy-done.4
  9.3 0.0 copy-start.5
  9.3 16.5 %products.1 = (bf16[32,128,128]{2,1,0:T(8,128)(2,1)}, bf16[32,16,128]{2,1,0:T(8,128)(2,1)S(1)}, bf16[32,144,128]{2,1,0:T(8,128)(2,1)}, bf16[32,160,128]{2,1,0:T(...) custom-call(bf16[128,12288]{1,0:T(8,128)(2,1)} %bitcast.23, ...), custom_call_target="tpu_custom_call" | custom-call | tf_op jit(solution)/shard_map/products/pallas_call | solution.py:382
  25.8 1.3 %collective-permute-start.3 = (bf16[32,144,128]{2,1,0:T(8,128)(2,1)}, bf16[32,144,128]{2,1,0:T(8,128)(2,1)}, u32[]{:S(2)}, u32[]{:S(2)}) collective-permute-start(bf16[32,144,128]{2,1,0:T(8,128)(2,1)} %get-tuple-element.19.refs_11_), channel_id=1, source_target_pairs={{1,0},{2,1},{3,2},{4,3},{5,4},{6,5},{7,6},{8,7},{9,8},{10,9},{11,1... | collective-permute-start | bytes 3538952 | tf_op jit(solution)/shard_map/ppermute | solution.py:23
  27.1 9.9 %collective-permute-start.2 = (bf16[32,128,128]{2,1,0:T(8,128)(2,1)}, bf16[32,128,128]{2,1,0:T(8,128)(2,1)}, u32[]{:S(2)}, u32[]{:S(2)}) collective-permute-start(bf16[32,128,128]{2,1,0:T(8,128)(2,1)} %get-tuple-element.17.refs_8_), channel_id=1, source_target_pairs={{0,1},{1,2},{2,3},{3,4},{4,5},{5,6},{6,7},{7,8},{8,9},{9,10},{10,1... | collective-permute-start | bytes 3145736 | tf_op jit(solution)/shard_map/ppermute | solution.py:23
  37.0 0.0 copy-done.5
  37.0 0.1 copy.13
  37.1 0.2 rev.6.refs_14_
  37.3 1.3 %collective-permute-done.2.refs_10_ = bf16[32,128,128]{2,1,0:T(8,128)(2,1)} collective-permute-done((bf16[32,128,128]{2,1,0:T(8,128)(2,1)}, bf16[32,128,128]{2,1,0:T(8,128)(2,1)}, u32[]{:S(2)}, u32[]{:S(2)}) %collective-permute-start.2) | collective-permute-done | bytes 1048608 | tf_op jit(solution)/shard_map/ppermute | solution.py:23
  38.6 0.0 collective-permute-done.3.refs_12_
  38.6 39.8 %gradients.1 = (bf16[128,4096]{1,0:T(8,128)(2,1)}, bf16[128,12288]{1,0:T(8,128)(2,1)}, f32[32,40,128]{2,1,0:T(8,128)S(1)}) custom-call(bf16[128,12288]{1,0:T(8,128)(2,1)} %bitcast.26, bf16[128,12288]{1,0:T(8,128)(2,1)} %bitcast.27, bf16[128,12288]{1,0:T(8,128)(2,1)} %bitcast.28, bf16[128,4096]{1,0:T(8,128)(2,1)S(1)} %bitcast.20, ...), custom_call_target="tpu_custom_call" | custom-call | tf_op jit(solution)/shard_map/gradients/pallas_call | solution.py:406
  78.5 37.1 %all_to_all.5 = f32[32,33,128]{2,1,0:T(8,128)S(1)} all-to-all(f32[32,33,128]{2,1,0:T(8,128)S(1)} %bitcast.22), channel_id=1, replica_groups=mesh['dp'=4,'seq'=32] {'seq'}, dimensions={0} | all-to-all | bytes 1081344 | tf_op jit(solution)/shard_map/all_to_all | solution.py:442
  115.5 0.1 reduce_sum.9
  115.6 3.1 %collective-permute-start.5 = (f32[33,128]{1,0:T(8,128)S(1)}, f32[33,128]{1,0:T(8,128)S(1)}, u32[]{:S(2)}, u32[]{:S(2)}) collective-permute-start(f32[33,128]{1,0:T(8,128)S(1)} %broadcast_multiply_fusion), channel_id=1, source_target_pairs={{0,64},{32,96},{64,0},{96,32},{1,65},{33,97},{65,1},{97,33},{2,66}... | collective-permute-start | bytes 50696 | tf_op jit(solution)/shard_map/ppermute | solution.py:445
  118.7 1.1 collective-permute-start.6
  119.8 0.9 collective-permute-start.4
  120.7 0.2 collective-permute-done.5
  121.0 1.5 %collective-permute-done.6 = f32[33,128]{1,0:T(8,128)S(1)} collective-permute-done((f32[33,128]{1,0:T(8,128)S(1)}, f32[33,128]{1,0:T(8,128)S(1)}, u32[]{:S(2)}, u32[]{:S(2)}) %collective-permute-start.6) | collective-permute-done | bytes 16928 | tf_op jit(solution)/shard_map/ppermute | solution.py:445
  122.5 2.4 %collective-permute-done.4 = f32[33,128]{1,0:T(8,128)S(1)} collective-permute-done((f32[33,128]{1,0:T(8,128)S(1)}, f32[33,128]{1,0:T(8,128)S(1)}, u32[]{:S(2)}, u32[]{:S(2)}) %collective-permute-start.4) | collective-permute-done | bytes 16928 | tf_op jit(solution)/shard_map/ppermute | solution.py:445
  124.8 0.6 slice.62
  125.5 0.6 reshape.24
  126.1 0.7 rev.7
  126.7 0.6 reshape.23
  (6 shorter events, 0.1 us)
Async XLA Ops:
  0.6 1.5 %copy-start.2 = (bf16[1,128,4096]{2,1,0:T(8,128)(2,1)S(1)}, bf16[1,128,4096]{2,1,0:T(8,128)(2,1)}, u32[]{:S(2)}) copy-start(bf16[1,128,4096]{2,1,0:T(8,128)(2,1)} %param.9) | copy-start | bytes 3145732
  3.1 6.2 %copy-start = (f32[3,12288]{1,0:T(4,128)S(1)}, f32[3,12288]{1,0:T(4,128)}, u32[]{:S(2)}) copy-start(f32[3,12288]{1,0:T(4,128)} %refs_22_.1) | copy-start | bytes 442372
  3.1 6.2 %copy-start.1 = (f32[3,12288]{1,0:T(4,128)S(1)}, f32[3,12288]{1,0:T(4,128)}, u32[]{:S(2)}) copy-start(f32[3,12288]{1,0:T(4,128)} %refs_26_.1) | copy-start | bytes 442372
  3.1 6.1 %copy-start.3 = (bf16[1,128,4096]{2,1,0:T(8,128)(2,1)S(1)}, bf16[1,128,4096]{2,1,0:T(8,128)(2,1)}, u32[]{:S(2)}) copy-start(bf16[1,128,4096]{2,1,0:T(8,128)(2,1)} %param.7) | copy-start | bytes 3145732
  3.1 6.1 %copy-start.4 = (f32[7,4096]{1,0:T(8,128)S(1)}, f32[7,4096]{1,0:T(8,128)}, u32[]{:S(2)}) copy-start(f32[7,4096]{1,0:T(8,128)} %refs_23_.1) | copy-start | bytes 344068
  3.2 6.0 %collective-permute-start.1 = (bf16[10,20480]{1,0:T(8,128)(2,1)S(1)}, bf16[10,20480]{1,0:T(8,128)(2,1)S(1)}, u32[]{:S(2)}, u32[]{:S(2)}) collective-permute-start(bf16[10,20480]{1,0:T(8,128)(2,1)S(1)} %pad_maximum_fusion), channel_id=1, source_target_pairs={{1,0},{2,1},{3,2},{4,3},{5,4},{6,5},{7,6},{8,7},{9,8},{10,9},{11,1... | collective-permute-start | bytes 1228808 | tf_op jit(solution)/shard_map/ppermute | solution.py:23
  4.7 4.6 %collective-permute-start = (bf16[10,16384]{1,0:T(8,128)(2,1)S(1)}, bf16[10,16384]{1,0:T(8,128)(2,1)S(1)}, u32[]{:S(2)}, u32[]{:S(2)}) collective-permute-start(bf16[10,16384]{1,0:T(8,128)(2,1)S(1)} %pad_maximum_fusion.1), channel_id=1, source_target_pairs={{0,1},{1,2},{2,3},{3,4},{4,5},{5,6},{6,7},{7,8},{8,9},{9,10},{10,1... | collective-permute-start | bytes 983048 | tf_op jit(solution)/shard_map/ppermute | solution.py:23
  9.3 27.7 %copy-start.5 = (bf16[128,256]{1,0:T(8,128)(2,1)S(1)}, bf16[128,256]{1,0:T(8,128)(2,1)}, u32[]{:S(2)}) copy-start(bf16[128,256]{1,0:T(8,128)(2,1)} %param.13) | copy-start | bytes 196612
  25.8 12.8 %collective-permute-start.3 = (bf16[32,144,128]{2,1,0:T(8,128)(2,1)}, bf16[32,144,128]{2,1,0:T(8,128)(2,1)}, u32[]{:S(2)}, u32[]{:S(2)}) collective-permute-start(bf16[32,144,128]{2,1,0:T(8,128)(2,1)} %get-tuple-element.19.refs_11_), channel_id=1, source_target_pairs={{1,0},{2,1},{3,2},{4,3},{5,4},{6,5},{7,6},{8,7},{9,8},{10,9},{11,1... | collective-permute-start | bytes 3538952 | tf_op jit(solution)/shard_map/ppermute | solution.py:23
  27.1 11.5 %collective-permute-start.2 = (bf16[32,128,128]{2,1,0:T(8,128)(2,1)}, bf16[32,128,128]{2,1,0:T(8,128)(2,1)}, u32[]{:S(2)}, u32[]{:S(2)}) collective-permute-start(bf16[32,128,128]{2,1,0:T(8,128)(2,1)} %get-tuple-element.17.refs_8_), channel_id=1, source_target_pairs={{0,1},{1,2},{2,3},{3,4},{4,5},{5,6},{6,7},{7,8},{8,9},{9,10},{10,1... | collective-permute-start | bytes 3145736 | tf_op jit(solution)/shard_map/ppermute | solution.py:23
  115.6 5.4 %collective-permute-start.5 = (f32[33,128]{1,0:T(8,128)S(1)}, f32[33,128]{1,0:T(8,128)S(1)}, u32[]{:S(2)}, u32[]{:S(2)}) collective-permute-start(f32[33,128]{1,0:T(8,128)S(1)} %broadcast_multiply_fusion), channel_id=1, source_target_pairs={{0,64},{32,96},{64,0},{96,32},{1,65},{33,97},{65,1},{97,33},{2,66}... | collective-permute-start | bytes 50696 | tf_op jit(solution)/shard_map/ppermute | solution.py:445
  118.7 3.8 %collective-permute-start.6 = (f32[33,128]{1,0:T(8,128)S(1)}, f32[33,128]{1,0:T(8,128)S(1)}, u32[]{:S(2)}, u32[]{:S(2)}) collective-permute-start(f32[33,128]{1,0:T(8,128)S(1)} %broadcast_multiply_fusion), channel_id=1, source_target_pairs={{0,96},{32,0},{64,32},{96,64},{1,97},{33,1},{65,33},{97,65},{2,98}... | collective-permute-start | bytes 50696 | tf_op jit(solution)/shard_map/ppermute | solution.py:445
  119.8 5.0 %collective-permute-start.4 = (f32[33,128]{1,0:T(8,128)S(1)}, f32[33,128]{1,0:T(8,128)S(1)}, u32[]{:S(2)}, u32[]{:S(2)}) collective-permute-start(f32[33,128]{1,0:T(8,128)S(1)} %broadcast_multiply_fusion), channel_id=1, source_target_pairs={{0,32},{32,64},{64,96},{96,0},{1,33},{33,65},{65,97},{97,1},{2,34}... | collective-permute-start | bytes 50696 | tf_op jit(solution)/shard_map/ppermute | solution.py:445

commit v2 on v1

v2 whole, which is shorter than its diff:
```python
import functools
import math

import jax
import jax.numpy as jnp
from jax import lax
from jax.experimental import pallas as pl
from jax.experimental.pallas import tpu as pltpu
from jax.sharding import PartitionSpec as P

F32 = jnp.float32
BF16 = jnp.bfloat16
LANES = 128
GROUP = 16
GROUPS = LANES // GROUP
SPAN = 32
BLOCKS = LANES // SPAN
JOINED = SPAN // GROUP
EDGE = 10
FRAME = 24
BANDS = 64
TILES = 4


def shift_rows(array, axis, by):
    peers = lax.axis_size(axis)
    return lax.ppermute(array, axis, [(i, i + by) for i in range(peers) if 0 <= i + by < peers])


def lane_blocks(shape):
    return lax.broadcasted_iota(jnp.int32, shape, 1) // SPAN


def swap_blocks(parts):
    parts = list(parts)
    block = lane_blocks(parts[0].shape)
    step = BLOCKS // 2
    while step:
        low = (block & step) == 0
        shift = SPAN * step
        for i in range(BLOCKS):
            if i & step == 0:
                first, second = parts[i], parts[i + step]
                parts[i] = jnp.where(low, first, pltpu.roll(second, shift, 1))
                parts[i + step] = jnp.where(low, pltpu.roll(first, LANES - shift, 1), second)
        step //= 2
    return parts


def taps_of(ref, lanes):
    return [ref[i : i + 1, lanes] for i in range(ref.shape[0])]


def back_taps(taps, ref, start, rows):
    total = taps[0] * ref[start : start + rows, :]
    for i in range(1, len(taps)):
        total = total + taps[i] * ref[start - i : start - i + rows, :]
    return total


def ahead_taps(taps, ref, start, rows):
    total = taps[0] * ref[start : start + rows, :]
    for i in range(1, len(taps)):
        total = total + taps[i] * ref[start + i : start + i + rows, :]
    return total


def first_kernel(rows, *refs):
    (q, k, v, res, g, pq, pk, pv, pr, nq, nk, nv, nr, ng) = refs[:14]
    (fsq, fsk, fsv, short, fmq, fmk, fmv) = refs[14:21]
    (w_own, w_edge, d_own, mid_out, q1_out, s1_out, k1_out, v1_out) = refs[21:29]
    (sq, sk, sv, sr, sg, sw, sm) = refs[29:]
    total = rows + GROUP

    @pl.when(pl.program_id(0) == 0)
    def _():
        for ref in (sq, sk, sv, sr, sg):
            ref[...] = jnp.zeros(ref.shape, F32)

    def one_tile(i, carry):
        lanes = pl.ds(pl.multiple_of(i * LANES, LANES), LANES)
        for scratch, own, before, after in (
            (sq, q, pq, nq),
            (sk, k, pk, nk),
            (sv, v, pv, nv),
            (sr, res, pr, nr),
            (sg, g, None, ng),
        ):
            if before is not None:
                scratch[FRAME - EDGE : FRAME, :] = before[:, lanes].astype(F32)
            for r in range(0, rows, GROUP):
                scratch[FRAME + r : FRAME + r + GROUP, :] = own[r : r + GROUP, lanes].astype(F32)
            scratch[FRAME + rows : FRAME + rows + EDGE, :] = after[:, lanes].astype(F32)
        tq, tk, tv = taps_of(fsq, lanes), taps_of(fsk, lanes), taps_of(fsv, lanes)
        for t in range(-GROUP, total, GROUP):
            at = FRAME + t
            k1 = back_taps(tk, sk, at, GROUP)
            v1 = back_taps(tv, sv, at, GROUP)
            sw[at : at + GROUP, :] = k1 * v1
            k1_out[i, t + GROUP : t + 2 * GROUP, :] = k1.astype(BF16)
            v1_out[i, t + GROUP : t + 2 * GROUP, :] = v1.astype(BF16)
        ts = taps_of(short, lanes)
        for t in range(-GROUP, total, GROUP):
            at = FRAME + t
            q1 = back_taps(tq, sq, at, GROUP)
            s1 = back_taps(ts, sw, at, GROUP)
            mid = (sr[at : at + GROUP, :] + q1 * s1).astype(BF16)
            sm[at : at + GROUP, :] = mid.astype(F32)
            mid_out[i, t + GROUP : t + 2 * GROUP, :] = mid
            if t >= 0:
                q1_out[i, t : t + GROUP, :] = q1.astype(BF16)
                s1_out[i, t : t + GROUP, :] = s1.astype(BF16)
        mq, mk, mv = taps_of(fmq, lanes), taps_of(fmk, lanes), taps_of(fmv, lanes)
        products, slopes = [], []
        for t in range(0, total, GROUP):
            at = FRAME + t
            m = [sm[at - j : at - j + GROUP, :] for j in range(3)]
            q2, k2, v2 = [
                taps[0] * m[0] + taps[1] * m[1] + taps[2] * m[2] for taps in (mq, mk, mv)
            ]
            products.append((k2 * v2).astype(BF16))
            slopes.append((sg[at : at + GROUP, :] * q2).astype(BF16))
        for values, own in ((products, w_own), (slopes, d_own)):
            parts = [
                jnp.concatenate(values[j : j + JOINED], 0)
                for j in range(0, GROUPS, JOINED)
            ]
            for j, part in enumerate(swap_blocks(parts)):
                own[i, j * SPAN : (j + 1) * SPAN, :] = part
        w_edge[i] = products[GROUPS]
        d_own[i, rows : rows + GROUP, :] = slopes[GROUPS]
        return carry

    lax.fori_loop(0, TILES, one_tile, 0)


def windows(low, high, last, block):
    rows = []
    for k in range(BLOCKS + 1):
        if k == 0:
            first, second = low, high
        elif k == BLOCKS:
            first, second = high, last
        else:
            shift = LANES - SPAN * k
            second = pltpu.roll(high, shift, 1)
            first = jnp.where(block < BLOCKS - k, pltpu.roll(low, shift, 1), second)
        rows.append(jnp.concatenate([first, second], 1))
    return jnp.concatenate(rows, 0)


def fold_diagonals(parts):
    row = lax.broadcasted_iota(jnp.int32, parts[0].shape, 0)
    half = len(parts) // 2
    while half:
        first = (row & half) == 0
        folded = []
        for x, y in zip(parts[:half], parts[half:]):
            low = jnp.where(first, x, pltpu.roll(y, half, 0))
            high = jnp.where(first, pltpu.roll(x, 8 - half, 0), y)
            folded.append(low + pltpu.roll(high, LANES - half, 1))
        parts = folded
        half //= 2
    return parts[0]


def fold_rows(parts):
    row = lax.broadcasted_iota(jnp.int32, parts[0].shape, 0)
    half = len(parts) // 2
    while half:
        first = (row & half) == 0
        parts = [
            jnp.where(first, x, pltpu.roll(y, half, 0))
            + jnp.where(first, pltpu.roll(x, 8 - half, 0), y)
            for x, y in zip(parts[:half], parts[half:])
        ]
        half //= 2
    return parts[0]


def toeplitz_kernel(taps_fwd, taps_rev, lag_out, ahead_out):
    shape = (SPAN, LANES)
    for j in range(BANDS):
        part = slice(j * SPAN, (j + 1) * SPAN)
        for taps, first, out in ((taps_fwd, 0, ahead_out), (taps_rev, 1, lag_out)):
            turned = pltpu.roll(
                jnp.broadcast_to(taps[j : j + 1, :], shape), first, 1, stride=1, stride_axis=0
            )
            out[part, :] = turned.astype(BF16)


def second_kernel(rows, channels, *refs):
    (q, k, v, g, pq, pk, pv, ng) = refs[:8]
    (w_own, w_edge, w_prev, d_own, d_next, lag_in, ahead_in) = refs[8:15]
    (mid_in, q1_in, s1_in, k1_in, v1_in) = refs[15:20]
    (fsq, fsk, fsv, short, fmq, fmk, fmv) = refs[20:27]
    (grad_res, grad_streams, sums_out) = refs[27:30]
    (sq, sk, sv, sg, sm, sw, dq, dk, dv, d1, eq, ek, ev) = refs[30:43]
    (s2_apart, w2_apart, s2_ends, w2_ends, s2_nat, w2_nat, diagonals, wins, d_wins) = refs[43:52]
    (s2_raw, w2_raw, acc, sums, moved, out_buf, sems) = refs[52:]
    now = pl.program_id(0)
    steps = pl.num_programs(0) - 1
    step = now - 1
    slot = lax.rem(now + 1, 2)
    width = TILES * LANES
    base = GROUP
    block = lane_blocks((SPAN, LANES))
    zero = jnp.zeros((), BF16)

    def copies(at_step, at_slot):
        return [
            pltpu.make_async_copy(
                out_buf.at[at_slot, x],
                grad_streams.at[
                    :, pl.ds(pl.multiple_of(x * channels + at_step * width, width), width)
                ],
                sems.at[at_slot, x],
            )
            for x in range(3)
        ]

    def lanes_of(i):
        return pl.ds(pl.multiple_of(i * LANES, LANES), LANES)

    def slot_of(n):
        return lax.broadcasted_iota(jnp.int32, (n, LANES), 1) // GROUP % JOINED

    def pick(wide, count, lanes):
        out = wide[:count, lanes]
        for n in range(1, JOINED):
            out = jnp.where(slot_of(count) == n, wide[n * SPAN : n * SPAN + count, lanes], out)
        return out

    def window_stage(i, j):
        part = slice(j * SPAN, (j + 1) * SPAN)
        no_rows = jnp.zeros((SPAN - GROUP, LANES), BF16)
        last_w = w_edge[i]
        last_d = d_next[i, rows : rows + GROUP, :]
        if j:
            last_w = pltpu.roll(last_w, LANES - SPAN * j, 1)
            last_d = pltpu.roll(last_d, LANES - SPAN * j, 1)
        for low, high, last, out in (
            (w_prev[i, part, :], w_own[i, part, :], last_w, wins),
            (d_own[i, part, :], d_next[i, part, :], last_d, d_wins),
        ):
            win = windows(low, high, jnp.concatenate([last, no_rows], 0), block)
            for n in range(2):
                out[n, :, j * LANES : (j + 1) * LANES] = win[:, n * LANES : (n + 1) * LANES]

    def filter_stage(i, j):
        taps_part = pl.ds((i * BLOCKS + j) * JOINED * SPAN, JOINED * SPAN)
        row = lax.broadcasted_iota(jnp.int32, (JOINED * SPAN, LANES), 0) % SPAN
        lane = lax.broadcasted_iota(jnp.int32, (JOINED * SPAN, LANES), 1)
        for bands, inside, win, raw in (
            (lag_in, lane > row, wins, s2_raw),
            (ahead_in, lane >= row, d_wins, w2_raw),
        ):
            at = slice(j * LANES, (j + 1) * LANES)
            turned = bands[taps_part, :]
            over = jnp.where(inside, zero, turned)[:, :SPAN]
            raw[j % 2] = jnp.dot(
                jnp.concatenate([jnp.where(inside, turned, zero), over], 1),
                jnp.concatenate([win[0, :, at], win[1, :, at]], 1),
                preferred_element_type=F32,
            )

    def pick_stage(j):
        part = slice(j * SPAN, (j + 1) * SPAN)
        main, edge = slice(0, LANES), slice(LANES, 2 * LANES)
        for raw, apart_ref, ends_ref in ((s2_raw, s2_apart, s2_ends), (w2_raw, w2_apart, w2_ends)):
            value = raw[j % 2].astype(BF16)
            apart_ref[part, :] = pick(value, SPAN, main)
            end = pick(value, GROUP, edge)
            ends_ref[j] = pltpu.roll(end, SPAN * j, 1) if j else end

    def cross_stage(i, first):
        row = lax.broadcasted_iota(jnp.int32, (SPAN, LANES), 0)
        lane = lax.broadcasted_iota(jnp.int32, (SPAN, LANES), 1)
        nothing = jnp.zeros((SPAN, LANES), BF16)
        apart = []
        for j in (first, first + 1):
            own_d = d_own[i, j * SPAN : (j + 1) * SPAN, :]
            for n in range(JOINED):
                mine = jnp.where(slot_of(SPAN) == n, own_d, zero)
                pair = [mine, nothing] if j == first else [nothing, mine]
                apart.append(jnp.concatenate(pair, 1))
        cross = lax.dot_general(
            jnp.concatenate(apart, 0),
            wins[0, :, first * LANES : (first + 2) * LANES],
            (((1,), (1,)), ((), ())),
            preferred_element_type=F32,
        )
        for n in range(2 * JOINED):
            mine = cross[n * SPAN : (n + 1) * SPAN]
            over = jnp.concatenate(
                [mine[:, LANES:], jnp.zeros((SPAN, LANES - SPAN), F32)], 1
            )
            mine = jnp.where(lane <= row, over, mine[:, :LANES])
            diagonals[first * JOINED + n] = sum(
                pltpu.roll(mine[r : r + 8], LANES - 1 - r, 1) for r in range(0, SPAN, 8)
            )

    def natural_stage(f):
        place = lax.rem(f + 2 * TILES, 2 * TILES)
        for apart_ref, ends_ref, nat in ((s2_apart, s2_ends, s2_nat), (w2_apart, w2_ends, w2_nat)):
            parts = swap_blocks([apart_ref[j * SPAN : (j + 1) * SPAN, :] for j in range(BLOCKS)])
            for j in range(BLOCKS):
                nat[place, j * SPAN : (j + 1) * SPAN, :] = parts[j]
            end = ends_ref[0]
            for j in range(1, BLOCKS):
                end = jnp.where(lane_blocks((GROUP, LANES)) == j, ends_ref[j], end)
            nat[place, rows : rows + GROUP, :] = end

    def fold_stage(f):
        sums[pl.ds(jnp.maximum(f, 0), 1), :GROUPS, :] = fold_diagonals(
            [diagonals[j] for j in range(GROUPS)]
        )[None]

    def input_stage(i):
        lanes = lanes_of(i)
        par = lax.rem(i, 2)
        for r in range(0, rows + 2 * GROUP, GROUP):
            sm[par, r : r + GROUP, :] = mid_in[i, r : r + GROUP, :].astype(F32)
        for r in range(0, rows + GROUP, GROUP):
            sw[par, r : r + GROUP, :] = k1_in[i, r : r + GROUP, :].astype(F32) * v1_in[
                i, r : r + GROUP, :
            ].astype(F32)
        for scratch, own, before in ((sq, q, pq), (sk, k, pk), (sv, v, pv)):
            scratch[par, base - EDGE : base, :] = before[:, lanes].astype(F32)
            for r in range(0, rows, GROUP):
                scratch[par, base + r : base + r + GROUP, :] = own[r : r + GROUP, lanes].astype(F32)
        sg[0:EDGE, :] = ng[:, lanes].astype(F32)

    def add_up(first, values, others, fresh):
        for n, other in enumerate(others):
            total = None
            for x, y in zip(values, other):
                product = x * y
                for r in range(0, GROUP, 8):
                    half = product[r : r + 8]
                    total = half if total is None else total + half
            acc[first + n] = total if fresh else acc[first + n] + total

    def element_stage(i, chunks):
        lanes = lanes_of(i)
        par = lax.rem(i, 2)
        place = lax.rem(step * TILES + i + 2 * TILES, 2 * TILES)
        main = chunks[0] < GROUPS
        fresh = chunks[0] == GROUPS - 1
        mq, mk, mv = taps_of(fmq, lanes), taps_of(fmk, lanes), taps_of(fmv, lanes)
        starts = [a * GROUP for a in chunks]
        at = lambda ref, t: ref[t : t + GROUP, :]
        gs = [g[t : t + GROUP, lanes].astype(F32) if main else sg[...] for t in starts]
        tall = lambda ref, t: ref[par, t : t + GROUP, :]
        mids = [[tall(sm, base + t - n) for t in starts] for n in range(3)]
        parts = [[], [], []]
        for c, t in enumerate(starts):
            m = [mids[n][c] for n in range(3)]
            k2 = mk[0] * m[0] + mk[1] * m[1] + mk[2] * m[2]
            v2 = mv[0] * m[0] + mv[1] * m[1] + mv[2] * m[2]
            s2 = s2_nat[place, t : t + GROUP, :].astype(F32)
            w2 = w2_nat[place, t : t + GROUP, :].astype(F32)
            for x, (ref, value) in enumerate(
                zip((dq, dk, dv), (gs[c] * s2, w2 * v2, w2 * k2))
            ):
                ref[t : t + GROUP, :] = value
                parts[x].append(value)
        if main:
            for x in range(3):
                add_up(9 + 3 * x, parts[x], mids, fresh)
        slopes = []
        for c, t in enumerate(starts):
            dmid = (
                gs[c]
                + ahead_taps(mq, dq, t, GROUP)
                + ahead_taps(mk, dk, t, GROUP)
                + ahead_taps(mv, dv, t, GROUP)
            )
            if main:
                grad_res[t : t + GROUP, lanes] = dmid.astype(BF16)
            slope = dmid * q1_in[i, t : t + GROUP, :].astype(F32)
            d1[t : t + GROUP, :] = slope
            slopes.append(slope)
            eq[t : t + GROUP, :] = dmid * s1_in[i, t : t + GROUP, :].astype(F32)
        ts = taps_of(short, lanes)
        if main:
            lagged = [[tall(sw, base + t - n) for t in starts] for n in range(len(ts))]
            add_up(18, slopes, lagged, fresh)
        for t in starts:
            dw1 = ahead_taps(ts, d1, t, GROUP)
            ek[t : t + GROUP, :] = dw1 * v1_in[i, base + t : base + t + GROUP, :].astype(F32)
            ev[t : t + GROUP, :] = dw1 * k1_in[i, base + t : base + t + GROUP, :].astype(F32)
        if not main:
            return
        for x, (ref, taps_ref, stream) in enumerate(((eq, fsq, sq), (ek, fsk, sk), (ev, fsv, sv))):
            taps = taps_of(taps_ref, lanes)
            for t in starts:
                out_buf[slot, x, t : t + GROUP, lanes] = ahead_taps(taps, ref, t, GROUP).astype(
                    BF16
                )
            add_up(
                3 * x,
                [at(ref, t) for t in starts],
                [[tall(stream, base + t - n) for t in starts] for n in range(3)],
                fresh,
            )

    def totals_stage(i):
        tile = pl.ds(jnp.maximum(step * TILES + i, 0), 1)
        for n in range(0, 24, 8):
            sums[tile, GROUPS + n : GROUPS + n + 8, :] = fold_rows(
                [acc[n + j] for j in range(8)]
            )[None]
        sums[tile, 32:33, :] = jnp.sum(acc[24], axis=0, keepdims=True)[None]

    @pl.when(now == 0)
    def _():
        for ref in (sg, dq, dk, dv, d1, eq, ek, ev):
            ref[...] = jnp.zeros(ref.shape, F32)

    @pl.when(step >= 2)
    def _():
        for copy in copies(step - 2, slot):
            copy.wait()

    def one_tile(filtering, differentiating):
        def run(i, carry):
            flat = now * TILES + i
            for j in reversed(range(BLOCKS)):

                @pl.when(i >= 0)
                def _():
                    if filtering:
                        if j == 3:
                            fold_stage(flat - 1)
                            pick_stage(0)
                        else:
                            if j == 2:
                                natural_stage(flat - 1)
                            pick_stage(j + 1)
                        filter_stage(i, j)
                        if j == 2:
                            cross_stage(i, 2)
                        if j == 0:
                            cross_stage(i, 0)
                        if j:
                            window_stage(i, j - 1)
                        else:
                            window_stage(jnp.minimum(i + 1, TILES - 1), BLOCKS - 1)
                    if differentiating:
                        element_stage(i, list(reversed(range(j * JOINED, (j + 1) * JOINED))))
                        if j == 1:
                            following = jnp.minimum(i + 1, TILES - 1)
                            input_stage(following)
                            element_stage(following, [GROUPS])
                        if j == 0:
                            totals_stage(i)

            return carry

        return run

    @pl.when(now == 0)
    def _():
        window_stage(0, BLOCKS - 1)
        lax.fori_loop(0, TILES, one_tile(True, False), 0)

    @pl.when(jnp.logical_and(now > 0, now < steps))
    def _():
        window_stage(0, BLOCKS - 1)
        input_stage(0)
        element_stage(0, [GROUPS])
        lax.fori_loop(0, TILES, one_tile(True, True), 0)

    @pl.when(now == steps)
    def _():
        fold_stage(now * TILES - 1)
        pick_stage(0)
        natural_stage(now * TILES - 1)
        input_stage(0)
        element_stage(0, [GROUPS])
        lax.fori_loop(0, TILES, one_tile(False, True), 0)

    @pl.when(step >= 0)
    def _():
        for copy in copies(step, slot):
            copy.start()

    @pl.when(now == steps)
    def _():
        tiles = sums.shape[0]
        for x in range(3):
            for tile in range(tiles):
                to, place = divmod(x * tiles + tile, 3)
                for n in range(3):
                    for row in (GROUPS, GROUPS + 9):
                        moved[to, row + 3 * n + place : row + 3 * n + place + 1, :] = sums[
                            tile, row + 3 * x + n : row + 3 * x + n + 1, :
                        ]
        for tile in range(tiles):
            moved[tile, :GROUPS, :] = sums[tile, :GROUPS, :]
            moved[tile, 26:33, :] = sums[tile, 26:33, :]
        sums_out[...] = moved[:, :33, :].astype(BF16)

        @pl.when(steps > 1)
        def _():
            for copy in copies(step - 1, 1 - slot):
                copy.wait()

        for copy in copies(step, slot):
            copy.wait()


def last_kernel(scale, first, second, third, fourth, fs_out, fm_out, short_out, medium_out):
    total = (first[...] + second[...] + third[...] + fourth[...]) * scale
    for out, row in ((fs_out, 8), (fm_out, 17)):
        for n in range(9):
            lanes = slice(n % 3 * LANES, (n % 3 + 1) * LANES)
            out[n // 3 : n // 3 + 1, lanes] = total[row + n : row + n + 1]
    short_out[...] = total[26:33]
    row = lax.broadcasted_iota(jnp.int32, (LANES, LANES), 0)
    lane = lax.broadcasted_iota(jnp.int32, (LANES, LANES), 1)
    flip = jnp.where(row + lane == LANES - 1, 1.0, 0.0).astype(F32)
    medium_out[...] = lax.dot_general(
        total[0:8],
        flip,
        (((1,), (1,)), ((), ())),
        precision=lax.Precision.HIGHEST,
        preferred_element_type=F32,
    )


def columns(rows, first=0):
    width = TILES * LANES
    return pl.BlockSpec((rows, width), lambda j: (0, first + j))


def moved_spec(spec, move):
    return pl.BlockSpec(spec.block_shape, lambda j: spec.index_map(move(j)))


def tiled(rows):
    return pl.BlockSpec((TILES, rows, LANES), lambda j: (j, 0, 0))


def shards(
    residual_in, se_streams, cotangent, feat_short, feat_medium, short_filter, medium_filter_weight
):
    res, streams, g = residual_in[0], se_streams[0], cotangent[0]
    rows, channels = res.shape
    seqs, slabs = lax.axis_size("seq"), lax.axis_size("dp")
    tiles = channels // LANES
    steps = tiles // TILES
    groups = medium_filter_weight.shape[1]
    before = shift_rows(
        jnp.concatenate([streams[rows - EDGE :], res[rows - EDGE :]], 1), "seq", 1
    )
    after = shift_rows(
        jnp.concatenate([streams[:EDGE], res[:EDGE], g[:EDGE]], 1), "seq", -1
    )
    edge = functools.partial(columns, EDGE)
    tap_specs = [columns(3, x * steps) for x in range(3)]
    filters = (feat_short,) * 3 + (short_filter,) + (feat_medium,) * 3
    filter_specs = tap_specs + [columns(short_filter.shape[0])] + tap_specs
    long, ext = rows + 2 * GROUP, rows + GROUP
    saved = [long, ext, ext, long, long]
    scratch = pltpu.VMEM((FRAME + ext, LANES), F32)
    w_own, w_edge, d_own, mid, q1, s1, k1, v1 = pl.pallas_call(
        functools.partial(first_kernel, rows),
        grid=(steps,),
        in_specs=[columns(rows, x * steps) for x in range(3)]
        + [columns(rows)] * 2
        + [edge(x * steps) for x in range(4)]
        + [edge(x * steps) for x in range(5)]
        + filter_specs,
        out_specs=[tiled(rows), tiled(GROUP), tiled(ext)] + [tiled(n) for n in saved],
        out_shape=[
            jax.ShapeDtypeStruct((tiles, n, LANES), BF16) for n in [rows, GROUP, ext] + saved
        ],
        scratch_shapes=[scratch] * 7,
        compiler_params=pltpu.CompilerParams(vmem_limit_bytes=48 * 1024 * 1024),
        name="products",
    )(
        *[streams] * 3, res, g, *[before] * 4, *[after] * 5, *filters
    )
    w_prev = shift_rows(w_own, "seq", 1)
    d_next = shift_rows(d_own, "seq", -1)
    taps_fwd = medium_filter_weight.T.astype(F32)
    taps_rev = taps_fwd[:, ::-1]
    bands = pl.BlockSpec((BANDS * SPAN, LANES), lambda j: (j, 0))
    lag, ahead = pl.pallas_call(
        toeplitz_kernel,
        grid=(groups // BANDS,),
        in_specs=[pl.BlockSpec((BANDS, LANES), lambda j: (j, 0))] * 2,
        out_specs=[bands] * 2,
        out_shape=[jax.ShapeDtypeStruct((groups * SPAN, LANES), BF16)] * 2,
        name="toeplitz",
    )(taps_fwd, taps_rev)
    per_step = pl.BlockSpec((TILES * GROUPS * SPAN, LANES), lambda j: (j, 0))
    row_buf = lambda n: pltpu.VMEM((n, LANES), F32)
    element_specs = (
        [columns(rows, x * steps) for x in range(3)]
        + [columns(rows)]
        + [edge(x * steps) for x in range(3)]
        + [edge(4 * steps)]
    )
    behind = lambda spec: moved_spec(spec, lambda j: jnp.maximum(j - 1, 0))
    ahead_of = lambda spec: moved_spec(spec, lambda j: jnp.minimum(j, steps - 1))
    grad_res, grad_streams, sums = pl.pallas_call(
        functools.partial(second_kernel, rows, channels),
        grid=(steps + 1,),
        in_specs=[behind(spec) for spec in element_specs]
        + [
            ahead_of(spec)
            for spec in [tiled(rows), tiled(GROUP), tiled(rows), tiled(ext), tiled(ext)]
            + [per_step] * 2
        ]
        + [behind(spec) for spec in [tiled(n) for n in saved] + filter_specs],
        out_specs=[
            behind(columns(rows)),
            pl.BlockSpec(memory_space=pl.ANY),
            pl.BlockSpec((tiles, 33, LANES), lambda j: (0, 0, 0)),
        ],
        out_shape=[
            jax.ShapeDtypeStruct((rows, channels), BF16),
            jax.ShapeDtypeStruct((rows, 3 * channels), BF16),
            jax.ShapeDtypeStruct((tiles, 33, LANES), BF16),
        ],
        scratch_shapes=[pltpu.VMEM((2, GROUP + rows, LANES), F32)] * 3
        + [row_buf(GROUP)] + [pltpu.VMEM((2, n, LANES), F32) for n in (long, ext)]
        + [row_buf(ext + 8)] * 7
        + [pltpu.VMEM((rows, LANES), BF16)] * 2
        + [pltpu.VMEM((BLOCKS, GROUP, LANES), BF16)] * 2
        + [pltpu.VMEM((2 * TILES, ext, LANES), BF16)] * 2
        + [pltpu.VMEM((GROUPS, 8, LANES), F32)]
        + [pltpu.VMEM((2, LANES + SPAN, BLOCKS * LANES), BF16)] * 2
        + [pltpu.VMEM((2, JOINED * SPAN, 2 * LANES), F32)] * 2
        + [
            pltpu.VMEM((25, 8, LANES), F32),
            pltpu.VMEM((tiles, 40, LANES), F32),
            pltpu.VMEM((tiles, 40, LANES), F32),
            pltpu.VMEM((2, 3, rows, TILES * LANES), BF16),
            pltpu.SemaphoreType.DMA((2, 3)),
        ],
        compiler_params=pltpu.CompilerParams(vmem_limit_bytes=48 * 1024 * 1024),
        name="gradients",
    )(
        *[streams] * 3, g, *[before] * 3, after,
        w_own, w_edge, w_prev, d_own, d_next, lag, ahead,
        mid, q1, s1, k1, v1, *filters
    )
    norm_factor = 1.0 / math.sqrt(slabs * seqs * rows)
    parts = lax.all_to_all(sums, "seq", split_axis=0, concat_axis=0, tiled=True)
    share = jnp.sum(parts.astype(F32), axis=0)
    others = [
        lax.ppermute(share, "dp", [(i, (i + n) % slabs) for i in range(slabs)])
        for n in range(1, slabs)
    ]
    cols = 3 * channels // tiles
    filter_grads = pl.pallas_call(
        functools.partial(last_kernel, norm_factor),
        out_shape=[
            jax.ShapeDtypeStruct(shape, F32)
            for shape in ((3, cols), (3, cols), (7, LANES), (GROUPS, LANES))
        ],
        name="totals",
    )(share, *others)
    return (grad_res[None], grad_streams[None], *filter_grads[:3], filter_grads[3].T)


def solution(mesh):
    placed = (P("dp", "seq", None), P("dp", "seq", None), P("dp", "seq", None), P(), P(), P(), P())
    return jax.shard_map(
        shards,
        mesh=mesh,
        in_specs=placed,
        out_specs=(
            P("dp", "seq", None),
            P("dp", "seq", None),
            P(None, "seq"),
            P(None, "seq"),
            P(None, "seq"),
            P(None, "seq"),
        ),
        check_vma=False,
    )
```

time: 128 us -> 111 us (0.87)
  Pallas kernels: 56.3 us -> 49.4 us
  blocking collectives: 37.1 us -> 30.4 us
  waiting for transfers between devices: 6.88 us -> 5.6 us
    pallas_call x1, Pallas kernels: 39.8 us -> 29.4 us  [shards(): pl.pallas_call(functools.partial(second_kernel, rows, channels), grid=(st...]
    all_to_all x1, blocking collectives: 37.1 us -> 30.4 us  [shards(): parts = lax.all_to_all(sums, 'seq', split_axis=0, concat_axis=0, tiled=True)]
    pallas_call x0 -> x2, Pallas kernels: none -> 5.77 us  [the longest x1 4.18 us: shards(): pl.pallas_call(toeplitz_kernel, grid=(groups // BANDS,), in_specs=[pl.Blo...]
    pallas_call x1, Pallas kernels: 16.5 us -> 14.2 us  [shards(): pl.pallas_call(functools.partial(first_kernel, rows), grid=(steps,), in_s...]
  transfers between devices with their start and end apart: 7 -> 7, of which waited for: 5 -> 3; matrix products, arithmetic and copies ran while one was open for 0% -> 1% of each run, Pallas kernels for 0% -> 4%
where the time goes in v2:
time: 111 us
  Pallas kernels  49.4 us (45%)
  blocking collectives  30.4 us (27%)
  starting transfers between devices  20.2 us (18%)
  waiting for transfers between devices  5.6 us (5%)
  local copies, waits for them, and re-layouts  4.13 us (4%)
    all_to_all x1, blocking collectives, shards(): parts = lax.all_to_all(sums, 'seq', split_axis=0, concat_axis=0, tiled=True)  30.4 us
    pallas_call x1, Pallas kernels, shards(): pl.pallas_call(functools.partial(second_kernel, rows, channels), grid=(st...  29.4 us
    ppermute x4, starting transfers between devices, shift_rows(): lax.ppermute(array, axis, [(i, i + by) for i in range(peers) if 0 <= i +...  15.7 us
    pallas_call x1, Pallas kernels, shards(): pl.pallas_call(functools.partial(first_kernel, rows), grid=(steps,), in_s...  14.2 us
    ppermute x3, starting transfers between devices, shards(): lax.ppermute(share, 'dp', [(i, (i + n) % slabs) for i in range(slabs)])  4.51 us
    pallas_call x1, Pallas kernels, shards(): pl.pallas_call(toeplitz_kernel, grid=(groups // BANDS,), in_specs=[pl.Blo...  4.18 us
    ppermute x3, waiting for transfers between devices, shards(): lax.ppermute(share, 'dp', [(i, (i + n) % slabs) for i in range(slabs)])  4.1 us
  transfers between devices with their start and end apart: 7, of which 3 were waited for; matrix products, arithmetic and copies ran while one was open for 1% of the time, Pallas kernels for 4%

profile of v2, /device:TPU:0, one launch (start us, length us, event | category | flops | bytes accessed | tf_op | source)
XLA Modules:
  0.0 110.6 jit_solution(7785407508810685151)
XLA Ops:
  0.6 0.0 copy-start.2
  0.6 1.3 %slice_bitcast_fusion = (bf16[10,12288]{1,0:T(8,128)(2,1)S(1)}, bf16[10,12288]{1,0:T(8,128)(2,1)S(1)}) fusion(bf16[1,128,12288]{2,1,0:T(8,128)(2,1)} %param.8), kind=kLoop, calls=%fused_computation.3 | loop fusion | bytes 983040 | tf_op jit(solution)/shard_map/slice | solution.py:559
  1.9 0.2 copy-done.2
  2.1 1.0 slice_bitcast_fusion.3
  3.1 0.0 copy-start
  3.1 0.0 copy-start.1
  3.1 0.0 copy-start.3
  3.1 0.0 copy-start.4
  3.1 0.1 pad_maximum_fusion
  3.2 1.4 %collective-permute-start.1 = (bf16[10,20480]{1,0:T(8,128)(2,1)S(1)}, bf16[10,20480]{1,0:T(8,128)(2,1)S(1)}, u32[]{:S(2)}, u32[]{:S(2)}) collective-permute-start(bf16[10,20480]{1,0:T(8,128)(2,1)S(1)} %pad_maximum_fusion), channel_id=1, source_target_pairs={{1,0},{2,1},{3,2},{4,3},{5,4},{6,5},{7,6},{8,7},{9,8},{10,9},{11,1... | collective-permute-start | bytes 1228808 | tf_op jit(solution)/shard_map/ppermute | solution.py:27
  4.7 3.1 %collective-permute-start = (bf16[10,16384]{1,0:T(8,128)(2,1)S(1)}, bf16[10,16384]{1,0:T(8,128)(2,1)S(1)}, u32[]{:S(2)}, u32[]{:S(2)}) collective-permute-start(bf16[10,16384]{1,0:T(8,128)(2,1)S(1)} %pad_maximum_fusion.1), channel_id=1, source_target_pairs={{0,1},{1,2},{2,3},{3,4},{4,5},{5,6},{6,7},{7,8},{8,9},{9,10},{10,1... | collective-permute-start | bytes 983048 | tf_op jit(solution)/shard_map/ppermute | solution.py:27
  7.8 1.5 %collective-permute-done.refs_5_.refs_6_.refs_7_.refs_8_.refs_4_ = bf16[10,16384]{1,0:T(8,128)(2,1)S(1)} collective-permute-done((bf16[10,16384]{1,0:T(8,128)(2,1)S(1)}, bf16[10,16384]{1,0:T(8,128)(2,1)S(1)}, u32[]{:S(2)}, u32[]{:S(2)}) %collective-permute-start) | collective-permute-done | bytes 327712 | tf_op jit(solution)/shard_map/ppermute | solution.py:27
  9.3 0.0 collective-permute-done.1.refs_9_.refs_10_.refs_11_.refs_12_.refs_13_.refs_7_
  9.3 0.0 copy-done
  9.3 0.0 copy-done.1
  9.3 0.0 copy-done.3
  9.3 0.0 copy-done.4
  9.3 0.0 copy-start.7
  9.3 14.2 %products.1 = (bf16[32,128,128]{2,1,0:T(8,128)(2,1)}, bf16[32,16,128]{2,1,0:T(8,128)(2,1)S(1)}, bf16[32,144,128]{2,1,0:T(8,128)(2,1)}, bf16[32,160,128]{2,1,0:T(...) custom-call(bf16[128,12288]{1,0:T(8,128)(2,1)} %bitcast.21, ...), custom_call_target="tpu_custom_call" | custom-call | tf_op jit(solution)/shard_map/products/pallas_call | solution.py:568
  23.5 1.3 %collective-permute-start.3 = (bf16[32,144,128]{2,1,0:T(8,128)(2,1)}, bf16[32,144,128]{2,1,0:T(8,128)(2,1)}, u32[]{:S(2)}, u32[]{:S(2)}) collective-permute-start(bf16[32,144,128]{2,1,0:T(8,128)(2,1)} %get-tuple-element.25.refs_11_), channel_id=1, source_target_pairs={{1,0},{2,1},{3,2},{4,3},{5,4},{6,5},{7,6},{8,7},{9,8},{10,9},{11,1... | collective-permute-start | bytes 3538952 | tf_op jit(solution)/shard_map/ppermute | solution.py:27
  24.8 9.9 %collective-permute-start.2 = (bf16[32,128,128]{2,1,0:T(8,128)(2,1)}, bf16[32,128,128]{2,1,0:T(8,128)(2,1)}, u32[]{:S(2)}, u32[]{:S(2)}) collective-permute-start(bf16[32,128,128]{2,1,0:T(8,128)(2,1)} %get-tuple-element.23.refs_8_), channel_id=1, source_target_pairs={{0,1},{1,2},{2,3},{3,4},{4,5},{5,6},{6,7},{7,8},{8,9},{9,10},{10,1... | collective-permute-start | bytes 3145736 | tf_op jit(solution)/shard_map/ppermute | solution.py:27
  34.7 0.0 copy-done.7
  34.7 0.1 copy.13
  34.8 0.0 copy-start.5
  34.8 0.8 rev.3.taps_rev
  35.7 0.0 copy-done.5
  35.7 4.2 %toeplitz.1 = (bf16[8192,128]{1,0:T(8,128)(2,1)}, bf16[8192,128]{1,0:T(8,128)(2,1)}) custom-call(f32[256,128]{1,0:T(8,128)} %copy-done.5, f32[256,128]{1,0:T(8,128)} %rev.3.taps_rev), custom_call_target="tpu_custom_call" | custom-call | tf_op jit(solution)/shard_map/toeplitz/pallas_call | solution.py:591
  39.9 0.0 collective-permute-done.2.refs_10_
  39.9 0.0 collective-permute-done.3.refs_12_
  39.9 29.4 %gradients.1 = (bf16[128,4096]{1,0:T(8,128)(2,1)}, bf16[128,12288]{1,0:T(8,128)(2,1)}, bf16[32,33,128]{2,1,0:T(8,128)(2,1)S(1)}) custom-call(bf16[128,12288]{1,0:T(8,128)(2,1)} %bitcast.24, bf16[128,12288]{1,0:T(8,128)(2,1)} %bitcast.25, bf16[128,12288]{1,0:T(8,128)(2,1)} %bitcast.26, bf16[128,4096]{1,0:T(8,128)(2,1)S(1)} %bitcast.19, ...), custom_call_target="tpu_custom_call" | custom-call | tf_op jit(solution)/shard_map/gradients/pallas_call | solution.py:609
  69.3 30.4 %all_to_all.5 = bf16[32,33,128]{2,1,0:T(8,128)(2,1)S(1)} all-to-all(bf16[32,33,128]{2,1,0:T(8,128)(2,1)S(1)} %get-tuple-element.35), channel_id=1, replica_groups=mesh['dp'=4,'seq'=32] {'seq'}, dimensions={0} | all-to-all | bytes 540672 | tf_op jit(solution)/shard_map/all_to_all | solution.py:653
  99.6 0.1 convert_reduce_fusion.first
  99.7 0.0 copy-start.6
  99.7 2.8 %collective-permute-start.6 = (f32[33,128]{1,0:T(8,128)S(1)}, f32[33,128]{1,0:T(8,128)S(1)}, u32[]{:S(2)}, u32[]{:S(2)}) collective-permute-start(f32[33,128]{1,0:T(8,128)S(1)} %convert_reduce_fusion.first), channel_id=1, source_target_pairs={{0,96},{32,0},{64,32},{96,64},{1,97},{33,1},{65,33},{97,65},{2,98}... | collective-permute-start | bytes 50696 | tf_op jit(solution)/shard_map/ppermute | solution.py:656
  102.5 0.8 collective-permute-start.5
  103.3 0.9 collective-permute-start.4
  104.2 0.0 collective-permute-done.6.fourth
  104.2 0.0 copy-start.8
  104.2 3.6 %collective-permute-done.5.third = f32[33,128]{1,0:T(8,128)S(1)} collective-permute-done((f32[33,128]{1,0:T(8,128)S(1)}, f32[33,128]{1,0:T(8,128)S(1)}, u32[]{:S(2)}, u32[]{:S(2)}) %collective-permute-start.5) | collective-permute-done | bytes 16928 | tf_op jit(solution)/shard_map/ppermute | solution.py:656
  107.8 0.0 copy-start.9
  107.8 0.5 collective-permute-done.4.second
  108.3 0.0 copy-done.6
  108.3 0.0 copy-done.8
  108.3 0.1 copy-done.9
  108.4 0.0 copy-start.10
  108.4 0.6 copy-done.10
  109.0 1.6 %totals.1 = (f32[3,384]{1,0:T(4,128)}, f32[3,384]{1,0:T(4,128)}, f32[7,128]{1,0:T(8,128)}, f32[8,128]{1,0:T(8,128)}) custom-call(f32[33,128]{1,0:T(8,128)} %copy-done.6, f32[33,128]{1,0:T(8,128)} %copy-done.10, f32[33,128]{1,0:T(8,128)} %copy-done.9, f32[33,128]{1,0:T(8,128)} %copy-done.8), custom_call_target="tpu_custom_call" | custom-call | tf_op jit(solution)/shard_map/totals/pallas_call | solution.py:660
  (2 shorter events, 0.1 us)
Async XLA Ops:
  0.6 1.5 %copy-start.2 = (bf16[1,128,4096]{2,1,0:T(8,128)(2,1)S(1)}, bf16[1,128,4096]{2,1,0:T(8,128)(2,1)}, u32[]{:S(2)}) copy-start(bf16[1,128,4096]{2,1,0:T(8,128)(2,1)} %param.9) | copy-start | bytes 3145732
  3.1 6.2 %copy-start = (f32[3,12288]{1,0:T(4,128)S(1)}, f32[3,12288]{1,0:T(4,128)}, u32[]{:S(2)}) copy-start(f32[3,12288]{1,0:T(4,128)} %refs_22_.1) | copy-start | bytes 442372
  3.1 6.2 %copy-start.1 = (f32[3,12288]{1,0:T(4,128)S(1)}, f32[3,12288]{1,0:T(4,128)}, u32[]{:S(2)}) copy-start(f32[3,12288]{1,0:T(4,128)} %refs_26_.1) | copy-start | bytes 442372
  3.1 6.1 %copy-start.3 = (bf16[1,128,4096]{2,1,0:T(8,128)(2,1)S(1)}, bf16[1,128,4096]{2,1,0:T(8,128)(2,1)}, u32[]{:S(2)}) copy-start(bf16[1,128,4096]{2,1,0:T(8,128)(2,1)} %param.7) | copy-start | bytes 3145732
  3.1 6.1 %copy-start.4 = (f32[7,4096]{1,0:T(8,128)S(1)}, f32[7,4096]{1,0:T(8,128)}, u32[]{:S(2)}) copy-start(f32[7,4096]{1,0:T(8,128)} %refs_23_.1) | copy-start | bytes 344068
  3.2 6.0 %collective-permute-start.1 = (bf16[10,20480]{1,0:T(8,128)(2,1)S(1)}, bf16[10,20480]{1,0:T(8,128)(2,1)S(1)}, u32[]{:S(2)}, u32[]{:S(2)}) collective-permute-start(bf16[10,20480]{1,0:T(8,128)(2,1)S(1)} %pad_maximum_fusion), channel_id=1, source_target_pairs={{1,0},{2,1},{3,2},{4,3},{5,4},{6,5},{7,6},{8,7},{9,8},{10,9},{11,1... | collective-permute-start | bytes 1228808 | tf_op jit(solution)/shard_map/ppermute | solution.py:27
  4.7 4.6 %collective-permute-start = (bf16[10,16384]{1,0:T(8,128)(2,1)S(1)}, bf16[10,16384]{1,0:T(8,128)(2,1)S(1)}, u32[]{:S(2)}, u32[]{:S(2)}) collective-permute-start(bf16[10,16384]{1,0:T(8,128)(2,1)S(1)} %pad_maximum_fusion.1), channel_id=1, source_target_pairs={{0,1},{1,2},{2,3},{3,4},{4,5},{5,6},{6,7},{7,8},{8,9},{9,10},{10,1... | collective-permute-start | bytes 983048 | tf_op jit(solution)/shard_map/ppermute | solution.py:27
  9.3 25.4 %copy-start.7 = (bf16[128,256]{1,0:T(8,128)(2,1)S(1)}, bf16[128,256]{1,0:T(8,128)(2,1)}, u32[]{:S(2)}) copy-start(bf16[128,256]{1,0:T(8,128)(2,1)} %param.13) | copy-start | bytes 196612
  23.5 16.4 %collective-permute-start.3 = (bf16[32,144,128]{2,1,0:T(8,128)(2,1)}, bf16[32,144,128]{2,1,0:T(8,128)(2,1)}, u32[]{:S(2)}, u32[]{:S(2)}) collective-permute-start(bf16[32,144,128]{2,1,0:T(8,128)(2,1)} %get-tuple-element.25.refs_11_), channel_id=1, source_target_pairs={{1,0},{2,1},{3,2},{4,3},{5,4},{6,5},{7,6},{8,7},{9,8},{10,9},{11,1... | collective-permute-start | bytes 3538952 | tf_op jit(solution)/shard_map/ppermute | solution.py:27
  24.8 15.1 %collective-permute-start.2 = (bf16[32,128,128]{2,1,0:T(8,128)(2,1)}, bf16[32,128,128]{2,1,0:T(8,128)(2,1)}, u32[]{:S(2)}, u32[]{:S(2)}) collective-permute-start(bf16[32,128,128]{2,1,0:T(8,128)(2,1)} %get-tuple-element.23.refs_8_), channel_id=1, source_target_pairs={{0,1},{1,2},{2,3},{3,4},{4,5},{5,6},{6,7},{7,8},{8,9},{9,10},{10,1... | collective-permute-start | bytes 3145736 | tf_op jit(solution)/shard_map/ppermute | solution.py:27
  34.8 0.8 copy-start.5
  99.7 8.6 %copy-start.6 = (f32[33,128]{1,0:T(8,128)}, f32[33,128]{1,0:T(8,128)S(1)}, u32[]{:S(2)}) copy-start(f32[33,128]{1,0:T(8,128)S(1)} %convert_reduce_fusion.first) | copy-start | bytes 50692
  99.7 4.5 %collective-permute-start.6 = (f32[33,128]{1,0:T(8,128)S(1)}, f32[33,128]{1,0:T(8,128)S(1)}, u32[]{:S(2)}, u32[]{:S(2)}) collective-permute-start(f32[33,128]{1,0:T(8,128)S(1)} %convert_reduce_fusion.first), channel_id=1, source_target_pairs={{0,96},{32,0},{64,32},{96,64},{1,97},{33,1},{65,33},{97,65},{2,98}... | collective-permute-start | bytes 50696 | tf_op jit(solution)/shard_map/ppermute | solution.py:656
  102.5 5.3 %collective-permute-start.5 = (f32[33,128]{1,0:T(8,128)S(1)}, f32[33,128]{1,0:T(8,128)S(1)}, u32[]{:S(2)}, u32[]{:S(2)}) collective-permute-start(f32[33,128]{1,0:T(8,128)S(1)} %convert_reduce_fusion.first), channel_id=1, source_target_pairs={{0,64},{32,96},{64,0},{96,32},{1,65},{33,97},{65,1},{97,33},{2,66}... | collective-permute-start | bytes 50696 | tf_op jit(solution)/shard_map/ppermute | solution.py:656
  103.3 5.0 %collective-permute-start.4 = (f32[33,128]{1,0:T(8,128)S(1)}, f32[33,128]{1,0:T(8,128)S(1)}, u32[]{:S(2)}, u32[]{:S(2)}) collective-permute-start(f32[33,128]{1,0:T(8,128)S(1)} %convert_reduce_fusion.first), channel_id=1, source_target_pairs={{0,32},{32,64},{64,96},{96,0},{1,33},{33,65},{65,97},{97,1},{2,34}... | collective-permute-start | bytes 50696 | tf_op jit(solution)/shard_map/ppermute | solution.py:656
  104.2 4.1 %copy-start.8 = (f32[33,128]{1,0:T(8,128)}, f32[33,128]{1,0:T(8,128)S(1)}, u32[]{:S(2)}) copy-start(f32[33,128]{1,0:T(8,128)S(1)} %collective-permute-done.6.fourth) | copy-start | bytes 50692
  107.8 0.6 copy-start.9
  108.4 0.6 copy-start.10

commit v3 on v2

--- a/solution.py
+++ b/solution.py
@@ -17,14 +17,18 @@
 BLOCKS = LANES // SPAN
 JOINED = SPAN // GROUP
 EDGE = 10
+EARLIER_ROWS = ((20, 4), (0, 10), (10, 10), (24, 2))
+EARLIER = 26
+LATER = 5 * EDGE
+LATER_AT = 32
 FRAME = 24
-BANDS = 64
+HALVES = 1
 TILES = 4
 
 
-def shift_rows(array, axis, by):
+def turn(array, axis, by):
     peers = lax.axis_size(axis)
-    return lax.ppermute(array, axis, [(i, i + by) for i in range(peers) if 0 <= i + by < peers])
+    return lax.ppermute(array, axis, [(i, (i + by) % peers) for i in range(peers)])
 
 
 def lane_blocks(shape):
@@ -65,11 +69,23 @@
     return total
 
 
+def rim_kernel(lq, lk, lv, lr, fq, fk, fv, fr, fg, before, after, rim):
+    for c in range(0, before.shape[1], LANES):
+        lanes = slice(c, c + LANES)
+        for at, ref in ((16, lr), (14, lq), (10, lv), (0, lk)):
+            rim[at : at + GROUP, :] = ref[:, lanes].astype(F32)
+        before[:, lanes] = rim[GROUP - EDGE : GROUP - EDGE + EARLIER, :].astype(BF16)
+        for x, ref in enumerate((fq, fk, fv, fr, fg)):
+            at = LATER_AT + EDGE * x
+            rim[at : at + GROUP, :] = ref[:, lanes].astype(F32)
+        after[:, lanes] = rim[LATER_AT : LATER_AT + LATER, :].astype(BF16)
+
+
 def first_kernel(rows, *refs):
-    (q, k, v, res, g, pq, pk, pv, pr, nq, nk, nv, nr, ng) = refs[:14]
-    (fsq, fsk, fsv, short, fmq, fmk, fmv) = refs[14:21]
-    (w_own, w_edge, d_own, mid_out, q1_out, s1_out, k1_out, v1_out) = refs[21:29]
-    (sq, sk, sv, sr, sg, sw, sm) = refs[29:]
+    (q, k, v, res, g, before, after) = refs[:7]
+    (fsq, fsk, fsv, short, fmq, fmk, fmv, inner) = refs[7:15]
+    (w_own, w_edge, d_own, mid_out, q1_out, s1_out, k1_out, v1_out) = refs[15:23]
+    (sq, sk, sv, sr, sg, sw, sm, rim) = refs[23:]
     total = rows + GROUP
 
     @pl.when(pl.program_id(0) == 0)
@@ -79,18 +95,16 @@
 
     def one_tile(i, carry):
         lanes = pl.ds(pl.multiple_of(i * LANES, LANES), LANES)
-        for scratch, own, before, after in (
-            (sq, q, pq, nq),
-            (sk, k, pk, nk),
-            (sv, v, pv, nv),
-            (sr, res, pr, nr),
-            (sg, g, None, ng),
-        ):
-            if before is not None:
-                scratch[FRAME - EDGE : FRAME, :] = before[:, lanes].astype(F32)
+        rim[0:EARLIER, :] = before[:, lanes].astype(F32) * inner[0]
+        rim[LATER_AT : LATER_AT + LATER, :] = after[:, lanes].astype(F32) * inner[1]
+        for x, (scratch, own) in enumerate(((sq, q), (sk, k), (sv, v), (sr, res), (sg, g))):
+            if x < 4:
+                at, count = EARLIER_ROWS[x]
+                scratch[FRAME - count : FRAME, :] = rim[at : at + count, :]
             for r in range(0, rows, GROUP):
                 scratch[FRAME + r : FRAME + r + GROUP, :] = own[r : r + GROUP, lanes].astype(F32)
-            scratch[FRAME + rows : FRAME + rows + EDGE, :] = after[:, lanes].astype(F32)
+            at = LATER_AT + EDGE * x
+            scratch[FRAME + rows : FRAME + rows + EDGE, :] = rim[at : at + EDGE, :]
         tq, tk, tv = taps_of(fsq, lanes), taps_of(fsk, lanes), taps_of(fsv, lanes)
         for t in range(-GROUP, total, GROUP):
             at = FRAME + t
@@ -178,9 +192,18 @@
     return parts[0]
 
 
-def toeplitz_kernel(taps_fwd, taps_rev, lag_out, ahead_out):
+def toeplitz_kernel(taps, lag_out, ahead_out, taps_fwd, taps_rev):
+    row = lax.broadcasted_iota(jnp.int32, (LANES, LANES), 0)
+    lane = lax.broadcasted_iota(jnp.int32, (LANES, LANES), 1)
+    for out, places in ((taps_fwd, row == lane), (taps_rev, row + lane == LANES - 1)):
+        out[...] = lax.dot_general(
+            taps[...],
+            jnp.where(places, 1.0, 0.0).astype(BF16),
+            (((0,), (0,)), ((), ())),
+            preferred_element_type=F32,
+        )
     shape = (SPAN, LANES)
-    for j in range(BANDS):
+    for j in range(LANES):
         part = slice(j * SPAN, (j + 1) * SPAN)
         for taps, first, out in ((taps_fwd, 0, ahead_out), (taps_rev, 1, lag_out)):
             turned = pltpu.roll(
@@ -189,12 +212,16 @@
             out[part, :] = turned.astype(BF16)
 
 
-def second_kernel(rows, channels, *refs):
-    (q, k, v, g, pq, pk, pv, ng) = refs[:8]
+def second_kernel(rows, channels, half, *refs):
+    (q, k, v, g, before, after) = refs[:6]
+    rim, refs = refs[-1], (None, None) + refs[:-1]
     (w_own, w_edge, w_prev, d_own, d_next, lag_in, ahead_in) = refs[8:15]
     (mid_in, q1_in, s1_in, k1_in, v1_in) = refs[15:20]
-    (fsq, fsk, fsv, short, fmq, fmk, fmv) = refs[20:27]
-    (grad_res, grad_streams, sums_out) = refs[27:30]
+    (fsq, fsk, fsv, short, fmq, fmk, fmv, inner) = refs[20:28]
+    if half:
+        earlier, refs = refs[28], refs[:28] + refs[31:]
+    (grad_res, grad_streams, sums_out) = refs[28:31]
+    refs = refs[:27] + refs[28:]
     (sq, sk, sv, sg, sm, sw, dq, dk, dv, d1, eq, ek, ev) = refs[30:43]
     (s2_apart, w2_apart, s2_ends, w2_ends, s2_nat, w2_nat, diagonals, wins, d_wins) = refs[43:52]
     (s2_raw, w2_raw, acc, sums, moved, out_buf, sems) = refs[52:]
@@ -212,7 +239,11 @@
             pltpu.make_async_copy(
                 out_buf.at[at_slot, x],
                 grad_streams.at[
-                    :, pl.ds(pl.multiple_of(x * channels + at_step * width, width), width)
+                    :,
+                    pl.ds(
+                        pl.multiple_of(x * channels + (half * steps + at_step) * width, width),
+                        width,
+                    ),
                 ],
                 sems.at[at_slot, x],
             )
@@ -234,14 +265,15 @@
     def window_stage(i, j):
         part = slice(j * SPAN, (j + 1) * SPAN)
         no_rows = jnp.zeros((SPAN - GROUP, LANES), BF16)
+        keep = [jnp.full((SPAN, LANES), inner[n], F32).astype(BF16) for n in range(2)]
         last_w = w_edge[i]
-        last_d = d_next[i, rows : rows + GROUP, :]
+        last_d = d_next[i, rows : rows + GROUP, :] * keep[1][:GROUP]
         if j:
             last_w = pltpu.roll(last_w, LANES - SPAN * j, 1)
             last_d = pltpu.roll(last_d, LANES - SPAN * j, 1)
         for low, high, last, out in (
-            (w_prev[i, part, :], w_own[i, part, :], last_w, wins),
-            (d_own[i, part, :], d_next[i, part, :], last_d, d_wins),
+            (w_prev[i, part, :] * keep[0], w_own[i, part, :], last_w, wins),
+            (d_own[i, part, :], d_next[i, part, :] * keep[1], last_d, d_wins),
         ):
             win = windows(low, high, jnp.concatenate([last, no_rows], 0), block)
             for n in range(2):
@@ -325,11 +357,14 @@
             sw[par, r : r + GROUP, :] = k1_in[i, r : r + GROUP, :].astype(F32) * v1_in[
                 i, r : r + GROUP, :
             ].astype(F32)
-        for scratch, own, before in ((sq, q, pq), (sk, k, pk), (sv, v, pv)):
-            scratch[par, base - EDGE : base, :] = before[:, lanes].astype(F32)
+        rim[0:EARLIER, :] = before[:, lanes].astype(F32) * inner[0]
+        rim[LATER_AT : LATER_AT + LATER, :] = after[:, lanes].astype(F32) * inner[1]
+        for x, (scratch, own) in enumerate(((sq, q), (sk, k), (sv, v))):
+            at, count = EARLIER_ROWS[x]
+            scratch[par, base - 2 : base, :] = rim[at + count - 2 : at + count, :]
             for r in range(0, rows, GROUP):
                 scratch[par, base + r : base + r + GROUP, :] = own[r : r + GROUP, lanes].astype(F32)
-        sg[0:EDGE, :] = ng[:, lanes].astype(F32)
+        sg[0:EDGE, :] = rim[LATER_AT + 4 * EDGE : LATER_AT + LATER, :]
 
     def add_up(first, values, others, fresh):
         for n, other in enumerate(others):
@@ -423,6 +458,22 @@
         for copy in copies(step - 2, slot):
             copy.wait()
 
+    def send_out():
+        tiles = sums.shape[0]
+        of = lambda tile: earlier if half and tile < tiles else sums
+        for to in range(moved.shape[0]):
+            for place in range(3):
+                x, tile = divmod(3 * to + place, moved.shape[0])
+                for n in range(3):
+                    for row in (GROUPS, GROUPS + 9):
+                        at, source = row + 3 * n + place, row + 3 * x + n
+                        moved[to, at : at + 1, :] = of(tile)[
+                            tile % tiles, source : source + 1, :
+                        ]
+            moved[to, :GROUPS, :] = of(to)[to % tiles, :GROUPS, :]
+            moved[to, 26:33, :] = of(to)[to % tiles, 26:33, :]
+        sums_out[...] = moved[:, :33, :].astype(BF16)
+
     def one_tile(filtering, differentiating):
         def run(i, carry):
             flat = now * TILES + i
@@ -488,19 +539,10 @@
 
     @pl.when(now == steps)
     def _():
-        tiles = sums.shape[0]
-        for x in range(3):
-            for tile in range(tiles):
-                to, place = divmod(x * tiles + tile, 3)
-                for n in range(3):
-                    for row in (GROUPS, GROUPS + 9):
-                        moved[to, row + 3 * n + place : row + 3 * n + place + 1, :] = sums[
-                            tile, row + 3 * x + n : row + 3 * x + n + 1, :
-                        ]
-        for tile in range(tiles):
-            moved[tile, :GROUPS, :] = sums[tile, :GROUPS, :]
-            moved[tile, 26:33, :] = sums[tile, 26:33, :]
-        sums_out[...] = moved[:, :33, :].astype(BF16)
+        if half == HALVES - 1:
+            send_out()
+        else:
+            sums_out[...] = sums[...]
 
         @pl.when(steps > 1)
         def _():
@@ -552,110 +594,144 @@
     tiles = channels // LANES
     steps = tiles // TILES
     groups = medium_filter_weight.shape[1]
-    before = shift_rows(
-        jnp.concatenate([streams[rows - EDGE :], res[rows - EDGE :]], 1), "seq", 1
-    )
-    after = shift_rows(
-        jnp.concatenate([streams[:EDGE], res[:EDGE], g[:EDGE]], 1), "seq", -1
-    )
-    edge = functools.partial(columns, EDGE)
-    tap_specs = [columns(3, x * steps) for x in range(3)]
+    cut = channels // 2
+    strip = lambda x, down: pl.BlockSpec((GROUP, cut), lambda j: (down, 2 * x + j))
+    last = rows // GROUP - 1
+    before, after = pl.pallas_call(
+        rim_kernel,
+        grid=(2,),
+        in_specs=[strip(x, last) for x in (0, 1, 2, 0)] + [strip(x, 0) for x in (0, 1, 2, 0, 0)],
+        out_specs=[pl.BlockSpec((n, cut), lambda j: (0, j)) for n in (EARLIER, LATER)],
+        out_shape=[jax.ShapeDtypeStruct((n, channels), BF16) for n in (EARLIER, LATER)],
+        scratch_shapes=[pltpu.VMEM((LATER_AT + LATER + 6, LANES), F32)],
+        compiler_params=pltpu.CompilerParams(vmem_limit_bytes=63 * 1024 * 1024),
+        name="rims",
+    )(*[streams] * 3, res, *[streams] * 3, res, g)
+    before, after = turn(before, "seq", 1), turn(after, "seq", -1)
+    seq = lax.axis_index("seq")
+    inner = jnp.stack([seq > 0, seq < seqs - 1]).astype(F32)
+    bands = pl.BlockSpec((LANES * SPAN, LANES), lambda j: (j, 0))
+    lag, ahead = pl.pallas_call(
+        toeplitz_kernel,
+        grid=(groups // LANES,),
+        in_specs=[pl.BlockSpec((LANES, LANES), lambda j: (0, j))],
+        out_specs=[bands] * 2,
+        out_shape=[jax.ShapeDtypeStruct((groups * SPAN, LANES), BF16)] * 2,
+        scratch_shapes=[pltpu.VMEM((LANES, LANES), F32)] * 2,
+        name="toeplitz",
+    )(medium_filter_weight)
+    inner, lag, ahead = lax.optimization_barrier((inner, lag, ahead))
+    half_tiles = tiles // HALVES
+    half_steps = half_tiles // TILES
     filters = (feat_short,) * 3 + (short_filter,) + (feat_medium,) * 3
-    filter_specs = tap_specs + [columns(short_filter.shape[0])] + tap_specs
     long, ext = rows + 2 * GROUP, rows + GROUP
     saved = [long, ext, ext, long, long]
+    in_smem = pl.BlockSpec(memory_space=pltpu.SMEM)
+    anywhere = pl.BlockSpec(memory_space=pl.ANY)
+    limit = pltpu.CompilerParams(vmem_limit_bytes=63 * 1024 * 1024)
     scratch = pltpu.VMEM((FRAME + ext, LANES), F32)
-    w_own, w_edge, d_own, mid, q1, s1, k1, v1 = pl.pallas_call(
-        functools.partial(first_kernel, rows),
-        grid=(steps,),
-        in_specs=[columns(rows, x * steps) for x in range(3)]
-        + [columns(rows)] * 2
-        + [edge(x * steps) for x in range(4)]
-        + [edge(x * steps) for x in range(5)]
-        + filter_specs,
-        out_specs=[tiled(rows), tiled(GROUP), tiled(ext)] + [tiled(n) for n in saved],
-        out_shape=[
-            jax.ShapeDtypeStruct((tiles, n, LANES), BF16) for n in [rows, GROUP, ext] + saved
-        ],
-        scratch_shapes=[scratch] * 7,
-        compiler_params=pltpu.CompilerParams(vmem_limit_bytes=48 * 1024 * 1024),
-        name="products",
-    )(
-        *[streams] * 3, res, g, *[before] * 4, *[after] * 5, *filters
-    )
-    w_prev = shift_rows(w_own, "seq", 1)
-    d_next = shift_rows(d_own, "seq", -1)
-    taps_fwd = medium_filter_weight.T.astype(F32)
-    taps_rev = taps_fwd[:, ::-1]
-    bands = pl.BlockSpec((BANDS * SPAN, LANES), lambda j: (j, 0))
-    lag, ahead = pl.pallas_call(
-        toeplitz_kernel,
-        grid=(groups // BANDS,),
-        in_specs=[pl.BlockSpec((BANDS, LANES), lambda j: (j, 0))] * 2,
-        out_specs=[bands] * 2,
-        out_shape=[jax.ShapeDtypeStruct((groups * SPAN, LANES), BF16)] * 2,
-        name="toeplitz",
-    )(taps_fwd, taps_rev)
-    per_step = pl.BlockSpec((TILES * GROUPS * SPAN, LANES), lambda j: (j, 0))
     row_buf = lambda n: pltpu.VMEM((n, LANES), F32)
-    element_specs = (
-        [columns(rows, x * steps) for x in range(3)]
-        + [columns(rows)]
-        + [edge(x * steps) for x in range(3)]
-        + [edge(4 * steps)]
-    )
     behind = lambda spec: moved_spec(spec, lambda j: jnp.maximum(j - 1, 0))
-    ahead_of = lambda spec: moved_spec(spec, lambda j: jnp.minimum(j, steps - 1))
-    grad_res, grad_streams, sums = pl.pallas_call(
-        functools.partial(second_kernel, rows, channels),
-        grid=(steps + 1,),
-        in_specs=[behind(spec) for spec in element_specs]
-        + [
-            ahead_of(spec)
-            for spec in [tiled(rows), tiled(GROUP), tiled(rows), tiled(ext), tiled(ext)]
-            + [per_step] * 2
-        ]
-        + [behind(spec) for spec in [tiled(n) for n in saved] + filter_specs],
-        out_specs=[
-            behind(columns(rows)),
-            pl.BlockSpec(memory_space=pl.ANY),
-            pl.BlockSpec((tiles, 33, LANES), lambda j: (0, 0, 0)),
-        ],
-        out_shape=[
-            jax.ShapeDtypeStruct((rows, channels), BF16),
-            jax.ShapeDtypeStruct((rows, 3 * channels), BF16),
-            jax.ShapeDtypeStruct((tiles, 33, LANES), BF16),
-        ],
-        scratch_shapes=[pltpu.VMEM((2, GROUP + rows, LANES), F32)] * 3
-        + [row_buf(GROUP)] + [pltpu.VMEM((2, n, LANES), F32) for n in (long, ext)]
-        + [row_buf(ext + 8)] * 7
-        + [pltpu.VMEM((rows, LANES), BF16)] * 2
-        + [pltpu.VMEM((BLOCKS, GROUP, LANES), BF16)] * 2
-        + [pltpu.VMEM((2 * TILES, ext, LANES), BF16)] * 2
-        + [pltpu.VMEM((GROUPS, 8, LANES), F32)]
-        + [pltpu.VMEM((2, LANES + SPAN, BLOCKS * LANES), BF16)] * 2
-        + [pltpu.VMEM((2, JOINED * SPAN, 2 * LANES), F32)] * 2
-        + [
-            pltpu.VMEM((25, 8, LANES), F32),
-            pltpu.VMEM((tiles, 40, LANES), F32),
-            pltpu.VMEM((tiles, 40, LANES), F32),
-            pltpu.VMEM((2, 3, rows, TILES * LANES), BF16),
-            pltpu.SemaphoreType.DMA((2, 3)),
-        ],
-        compiler_params=pltpu.CompilerParams(vmem_limit_bytes=48 * 1024 * 1024),
-        name="gradients",
-    )(
-        *[streams] * 3, g, *[before] * 3, after,
-        w_own, w_edge, w_prev, d_own, d_next, lag, ahead,
-        mid, q1, s1, k1, v1, *filters
-    )
+    ahead_of = lambda spec: moved_spec(spec, lambda j: jnp.minimum(j, half_steps - 1))
+
+    def specs_of(half):
+        block = lambda n: lambda x: columns(n, x * steps + half * half_steps)
+        filter_specs = (
+            [block(3)(x) for x in range(3)]
+            + [block(short_filter.shape[0])(0)]
+            + [block(3)(x) for x in range(3)]
+        )
+        return block(rows), [block(EARLIER)(0), block(LATER)(0)], filter_specs
+
+    def products(half):
+        whole, edge, filter_specs = specs_of(half)
+        return pl.pallas_call(
+            functools.partial(first_kernel, rows),
+            grid=(half_steps,),
+            in_specs=[whole(x) for x in range(3)]
+            + [whole(0)] * 2
+            + edge
+            + filter_specs
+            + [in_smem],
+            out_specs=[tiled(rows), tiled(GROUP), tiled(ext)] + [tiled(n) for n in saved],
+            out_shape=[
+                jax.ShapeDtypeStruct((half_tiles, n, LANES), BF16)
+                for n in [rows, GROUP, ext] + saved
+            ],
+            scratch_shapes=[scratch] * 7 + [row_buf(LATER_AT + LATER + 6)],
+            compiler_params=limit,
+            name="products",
+        )(*[streams] * 3, res, g, before, after, *filters, inner)
+
+    def gradients(half, made, w_prev, d_next, earlier):
+        whole, edge, filter_specs = specs_of(half)
+        w_own, w_edge, d_own, *kept = made
+        per_step = pl.BlockSpec(
+            (TILES * GROUPS * SPAN, LANES), lambda j: (half * half_steps + j, 0)
+        )
+        raw_sums = jax.ShapeDtypeStruct((half_tiles, 40, LANES), F32)
+        all_sums = jax.ShapeDtypeStruct((tiles, 33, LANES), BF16)
+        own_sums = pl.BlockSpec((half_tiles, 40, LANES), lambda j: (0, 0, 0))
+        own_shares = pl.BlockSpec((tiles, 33, LANES), lambda j: (0, 0, 0))
+        last = half == HALVES - 1
+        first_in = [whole(x) for x in range(3)] + [whole(0)] + edge
+        return pl.pallas_call(
+            functools.partial(second_kernel, rows, channels, half),
+            grid=(half_steps + 1,),
+            in_specs=[behind(spec) for spec in first_in]
+            + [
+                ahead_of(spec)
+                for spec in [tiled(rows), tiled(GROUP), tiled(rows), tiled(ext), tiled(ext)]
+                + [per_step] * 2
+            ]
+            + [behind(spec) for spec in [tiled(n) for n in saved] + filter_specs]
+            + [in_smem]
+            + ([own_sums, anywhere, anywhere] if half else []),
+            out_specs=[behind(whole(0)), anywhere] + [own_shares if last else own_sums],
+            out_shape=[
+                jax.ShapeDtypeStruct((rows, channels), BF16),
+                jax.ShapeDtypeStruct((rows, 3 * channels), BF16),
+            ]
+            + [all_sums if last else raw_sums],
+            input_output_aliases={27: 0, 28: 1} if half else {},
+            scratch_shapes=[pltpu.VMEM((2, GROUP + rows, LANES), F32)] * 3
+            + [row_buf(GROUP)]
+            + [pltpu.VMEM((2, n, LANES), F32) for n in (long, ext)]
+            + [row_buf(ext + 8)] * 7
+            + [pltpu.VMEM((rows, LANES), BF16)] * 2
+            + [pltpu.VMEM((BLOCKS, GROUP, LANES), BF16)] * 2
+            + [pltpu.VMEM((2 * TILES, ext, LANES), BF16)] * 2
+            + [pltpu.VMEM((GROUPS, 8, LANES), F32)]
+            + [pltpu.VMEM((2, LANES + SPAN, BLOCKS * LANES), BF16)] * 2
+            + [pltpu.VMEM((2, JOINED * SPAN, 2 * LANES), F32)] * 2
+            + [
+                pltpu.VMEM((25, 8, LANES), F32),
+                pltpu.VMEM((half_tiles, 40, LANES), F32),
+                pltpu.VMEM((tiles, 40, LANES), F32),
+                pltpu.VMEM((2, 3, rows, TILES * LANES), BF16),
+                pltpu.SemaphoreType.DMA((2, 3)),
+                row_buf(LATER_AT + LATER + 6),
+            ],
+            compiler_params=limit,
+            name="gradients",
+        )(
+            *[streams] * 3, g, before, after,
+            w_own, w_edge, w_prev, d_own, d_next, lag, ahead,
+            *kept, *filters, inner, *earlier
+        )
+
+    made, arrived = [], []
+    for half in range(HALVES):
+        made.append(products(half))
+        arrived.append((turn(made[half][0], "seq", 1), turn(made[half][2], "seq", -1)))
+    earlier = ()
+    for half in range(HALVES):
+        grad_res, grad_streams, sums = gradients(half, made[half], *arrived[half], earlier)
+        earlier = (sums, grad_res, grad_streams)
     norm_factor = 1.0 / math.sqrt(slabs * seqs * rows)
     parts = lax.all_to_all(sums, "seq", split_axis=0, concat_axis=0, tiled=True)
     share = jnp.sum(parts.astype(F32), axis=0)
-    others = [
-        lax.ppermute(share, "dp", [(i, (i + n) % slabs) for i in range(slabs)])
-        for n in range(1, slabs)
-    ]
+    others = [turn(share, "dp", n) for n in range(1, slabs)]
     cols = 3 * channels // tiles
     filter_grads = pl.pallas_call(
         functools.partial(last_kernel, norm_factor),

time: 111 us -> 108 us (0.973)
  waiting for transfers between devices: 5.6 us -> 27 us
  blocking collectives: 30.4 us -> 13.3 us
  starting transfers between devices: 20.2 us -> 12.1 us
  Pallas kernels: 49.4 us -> 51.9 us
  local copies, waits for them, and re-layouts: 4.13 us -> 2.19 us
    ppermute x7, waiting for transfers between devices: 5.6 us -> 27 us  [turn(): lax.ppermute(array, axis, [(i, (i + by) % peers) for i in range(peers)])]
    all_to_all x1, blocking collectives: 30.4 us -> 13.3 us  [shards(): parts = lax.all_to_all(sums, 'seq', split_axis=0, concat_axis=0, tiled=True)]
    ppermute x7, starting transfers between devices: 20.2 us -> 12.1 us  [turn(): lax.ppermute(array, axis, [(i, (i + by) % peers) for i in range(peers)])]
    pallas_call x3 -> x4, Pallas kernels: 47.8 us -> 50.3 us  [the longest x1 29.8 us: gradients(): pl.pallas_call(functools.partial(second_kernel, rows, channels, half), gr...]
    slice x2 -> x0, local copies, waits for them, and re-layouts: 2.29 us -> none  [the longest x1 1.3 us: shards(): streams[:EDGE]]
    unnamed x23 -> x12, local copies, waits for them, and re-layouts: 1.01 us -> 2.19 us
  transfers between devices with their start and end apart: 7 -> 7, of which waited for: 3 -> 4; matrix products, arithmetic and copies ran while one was open for 1% -> 1% of each run, Pallas kernels for 4% -> 3%
where the time goes in v3:
time: 108 us
  Pallas kernels  51.9 us (48%)
  waiting for transfers between devices  27 us (25%)
  blocking collectives  13.3 us (12%)
  starting transfers between devices  12.1 us (11%)
  local copies, waits for them, and re-layouts  2.19 us (2%)
    pallas_call x1, Pallas kernels, gradients(): pl.pallas_call(functools.partial(second_kernel, rows, channels, half), gr...  29.8 us
    ppermute x7, waiting for transfers between devices, turn(): lax.ppermute(array, axis, [(i, (i + by) % peers) for i in range(peers)])  27 us
    pallas_call x1, Pallas kernels, products(): pl.pallas_call(functools.partial(first_kernel, rows), grid=(half_steps,),...  14.5 us
    all_to_all x1, blocking collectives, shards(): parts = lax.all_to_all(sums, 'seq', split_axis=0, concat_axis=0, tiled=True)  13.3 us
    ppermute x7, starting transfers between devices, turn(): lax.ppermute(array, axis, [(i, (i + by) % peers) for i in range(peers)])  12.1 us
    pallas_call x1, Pallas kernels, shards(): pl.pallas_call(toeplitz_kernel, grid=(groups // LANES,), in_specs=[pl.Blo...  3.69 us
    pallas_call x1, Pallas kernels, shards(): pl.pallas_call(rim_kernel, grid=(2,), in_specs=[strip(x, last) for x in (...  2.28 us
    unnamed x12, local copies, waits for them, and re-layouts  2.19 us
  transfers between devices with their start and end apart: 7, of which 4 were waited for; matrix products, arithmetic and copies ran while one was open for 1% of the time, Pallas kernels for 3%

profile of v3, /device:TPU:0, one launch (start us, length us, event | category | flops | bytes accessed | tf_op | source)
XLA Modules:
  0.0 107.8 jit_solution(6545084379828581998)
XLA Ops:
  0.6 2.3 %rims.1 = (bf16[26,4096]{1,0:T(8,128)(2,1)}, bf16[50,4096]{1,0:T(8,128)(2,1)}) custom-call(bf16[128,12288]{1,0:T(8,128)(2,1)} %bitcast.8, bf16[128,12288]{1,0:T(8,128)(2,1)} %bitcast.9, bf16[128,12288]{1,0:T(8,128)(2,1)} %bitcast.10, bf16[128,4096]{1,0:T(8,128)(2,1)} %bitcast.23, bf16[128,12288]{1,0:T(8,128)(2,1)} %bitcast.11, bf16[128,12288]{1,0:T(8,128)(2,1)} %bitcast.12, ...), custom_call_target="tpu_custom_call" | custom-call | tf_op jit(solution)/shard_map/rims/pallas_call | solution.py:600
  2.9 6.1 %collective-permute-start.1 = (bf16[50,4096]{1,0:T(8,128)(2,1)}, bf16[50,4096]{1,0:T(8,128)(2,1)S(1)}, u32[]{:S(2)}, u32[]{:S(2)}) collective-permute-start(bf16[50,4096]{1,0:T(8,128)(2,1)} %get-tuple-element.29), channel_id=1, source_target_pairs={{0,31},{1,0},{2,1},{3,2},{4,3},{5,4},{6,5},{7,6},{8,7},{9,8},{10,9... | collective-permute-start | bytes 1228808 | tf_op jit(solution)/shard_map/ppermute | solution.py:31
  9.0 0.0 collective-permute-start
  9.0 3.7 %toeplitz.1 = (bf16[8192,128]{1,0:T(8,128)(2,1)}, bf16[8192,128]{1,0:T(8,128)(2,1)}) custom-call(bf16[128,256]{1,0:T(8,128)(2,1)} %taps.1), custom_call_target="tpu_custom_call" | custom-call | tf_op jit(solution)/shard_map/toeplitz/pallas_call | solution.py:614
  12.7 0.6 add_convert_fusion.refs_14_.refs_25_
  13.3 5.0 %collective-permute-done.refs_5_.refs_4_ = bf16[26,4096]{1,0:T(8,128)(2,1)S(1)} collective-permute-done((bf16[26,4096]{1,0:T(8,128)(2,1)}, bf16[26,4096]{1,0:T(8,128)(2,1)S(1)}, u32[]{:S(2)}, u32[]{:S(2)}) %collective-permute-start) | collective-permute-done | bytes 213024 | tf_op jit(solution)/shard_map/ppermute | solution.py:31
  18.3 0.0 copy-start.1
  18.3 0.0 collective-permute-done.1.refs_6_.refs_5_
  18.3 0.7 copy-done.1
  19.0 0.0 copy-start
  19.0 0.8 copy-done
  19.8 14.5 %products.1 = (bf16[32,128,128]{2,1,0:T(8,128)(2,1)}, bf16[32,16,128]{2,1,0:T(8,128)(2,1)}, bf16[32,144,128]{2,1,0:T(8,128)(2,1)}, bf16[32,160,128]{2,1,0:T(8,12...) custom-call(bf16[128,12288]{1,0:T(8,128)(2,1)} %bitcast.14, ...), custom_call_target="tpu_custom_call" | custom-call | tf_op jit(solution)/shard_map/products/pallas_call | solution.py:648
  34.3 1.5 %collective-permute-start.3 = (bf16[32,144,128]{2,1,0:T(8,128)(2,1)}, bf16[32,144,128]{2,1,0:T(8,128)(2,1)}, u32[]{:S(2)}, u32[]{:S(2)}) collective-permute-start(bf16[32,144,128]{2,1,0:T(8,128)(2,1)} %get-tuple-element.35.refs_9_), channel_id=1, source_target_pairs={{0,31},{1,0},{2,1},{3,2},{4,3},{5,4},{6,5},{7,6},{8,7},{9,8},{10,9... | collective-permute-start | bytes 3538952 | tf_op jit(solution)/shard_map/ppermute | solution.py:31
  35.8 0.0 collective-permute-start.2
  35.8 17.9 %collective-permute-done.2.refs_8_ = bf16[32,128,128]{2,1,0:T(8,128)(2,1)} collective-permute-done((bf16[32,128,128]{2,1,0:T(8,128)(2,1)}, bf16[32,128,128]{2,1,0:T(8,128)(2,1)}, u32[]{:S(2)}, u32[]{:S(2)}) %collective-permute-start.2) | collective-permute-done | bytes 1048608 | tf_op jit(solution)/shard_map/ppermute | solution.py:31
  53.7 0.0 collective-permute-done.3.refs_10_
  53.7 29.8 %gradients.1 = (bf16[128,4096]{1,0:T(8,128)(2,1)}, bf16[128,12288]{1,0:T(8,128)(2,1)}, bf16[32,33,128]{2,1,0:T(8,128)(2,1)}) custom-call(bf16[128,12288]{1,0:T(8,128)(2,1)} %bitcast.17, bf16[128,12288]{1,0:T(8,128)(2,1)} %bitcast.18, bf16[128,12288]{1,0:T(8,128)(2,1)} %bitcast.19, bf16[128,4096]{1,0:T(8,128)(2,1)} %bitcast.22, bf16[26,4096]{1,0:T(8,128)(2,1)} %copy-done.1, ...), custom_call_target="tpu_custom_call" | custom-call | tf_op jit(solution)/shard_map/gradients/pallas_call | solution.py:678
  83.5 13.3 %all_to_all.5 = bf16[32,33,128]{2,1,0:T(8,128)(2,1)S(1)} all-to-all(bf16[32,33,128]{2,1,0:T(8,128)(2,1)} %get-tuple-element.45), channel_id=1, replica_groups=mesh['dp'=4,'seq'=32] {'seq'}, dimensions={0} | all-to-all | bytes 540672 | tf_op jit(solution)/shard_map/all_to_all | solution.py:732
  96.8 0.1 convert_reduce_fusion.first
  96.9 0.0 copy-start.2
  96.9 2.8 %collective-permute-start.6 = (f32[33,128]{1,0:T(8,128)S(1)}, f32[33,128]{1,0:T(8,128)S(1)}, u32[]{:S(2)}, u32[]{:S(2)}) collective-permute-start(f32[33,128]{1,0:T(8,128)S(1)} %convert_reduce_fusion.first), channel_id=1, source_target_pairs={{0,96},{32,0},{64,32},{96,64},{1,97},{33,1},{65,33},{97,65},{2,98}... | collective-permute-start | bytes 50696 | tf_op jit(solution)/shard_map/ppermute | solution.py:31
  99.7 0.8 collective-permute-start.5
  100.5 0.9 collective-permute-start.4
  101.4 0.0 collective-permute-done.6.fourth
  101.4 0.0 copy-start.3
  101.4 3.6 %collective-permute-done.5.third = f32[33,128]{1,0:T(8,128)S(1)} collective-permute-done((f32[33,128]{1,0:T(8,128)S(1)}, f32[33,128]{1,0:T(8,128)S(1)}, u32[]{:S(2)}, u32[]{:S(2)}) %collective-permute-start.5) | collective-permute-done | bytes 16928 | tf_op jit(solution)/shard_map/ppermute | solution.py:31
  105.0 0.0 copy-start.4
  105.0 0.5 collective-permute-done.4.second
  105.5 0.0 copy-done.2
  105.5 0.0 copy-done.3
  105.5 0.1 copy-done.4
  105.6 0.0 copy-start.5
  105.6 0.6 copy-done.5
  106.2 1.6 %totals.1 = (f32[3,384]{1,0:T(4,128)}, f32[3,384]{1,0:T(4,128)}, f32[7,128]{1,0:T(8,128)}, f32[8,128]{1,0:T(8,128)}) custom-call(f32[33,128]{1,0:T(8,128)} %copy-done.2, f32[33,128]{1,0:T(8,128)} %copy-done.5, f32[33,128]{1,0:T(8,128)} %copy-done.4, f32[33,128]{1,0:T(8,128)} %copy-done.3), custom_call_target="tpu_custom_call" | custom-call | tf_op jit(solution)/shard_map/totals/pallas_call | solution.py:736
Async XLA Ops:
  2.9 15.4 %collective-permute-start.1 = (bf16[50,4096]{1,0:T(8,128)(2,1)}, bf16[50,4096]{1,0:T(8,128)(2,1)S(1)}, u32[]{:S(2)}, u32[]{:S(2)}) collective-permute-start(bf16[50,4096]{1,0:T(8,128)(2,1)} %get-tuple-element.29), channel_id=1, source_target_pairs={{0,31},{1,0},{2,1},{3,2},{4,3},{5,4},{6,5},{7,6},{8,7},{9,8},{10,9... | collective-permute-start | bytes 1228808 | tf_op jit(solution)/shard_map/ppermute | solution.py:31
  9.0 9.3 %collective-permute-start = (bf16[26,4096]{1,0:T(8,128)(2,1)}, bf16[26,4096]{1,0:T(8,128)(2,1)S(1)}, u32[]{:S(2)}, u32[]{:S(2)}) collective-permute-start(bf16[26,4096]{1,0:T(8,128)(2,1)} %get-tuple-element.28), channel_id=1, source_target_pairs={{0,1},{1,2},{2,3},{3,4},{4,5},{5,6},{6,7},{7,8},{8,9},{9,10},{10,1... | collective-permute-start | bytes 638984 | tf_op jit(solution)/shard_map/ppermute | solution.py:31
  18.3 0.7 copy-start.1
  19.0 0.8 copy-start
  34.3 19.3 %collective-permute-start.3 = (bf16[32,144,128]{2,1,0:T(8,128)(2,1)}, bf16[32,144,128]{2,1,0:T(8,128)(2,1)}, u32[]{:S(2)}, u32[]{:S(2)}) collective-permute-start(bf16[32,144,128]{2,1,0:T(8,128)(2,1)} %get-tuple-element.35.refs_9_), channel_id=1, source_target_pairs={{0,31},{1,0},{2,1},{3,2},{4,3},{5,4},{6,5},{7,6},{8,7},{9,8},{10,9... | collective-permute-start | bytes 3538952 | tf_op jit(solution)/shard_map/ppermute | solution.py:31
  35.8 17.9 %collective-permute-start.2 = (bf16[32,128,128]{2,1,0:T(8,128)(2,1)}, bf16[32,128,128]{2,1,0:T(8,128)(2,1)}, u32[]{:S(2)}, u32[]{:S(2)}) collective-permute-start(bf16[32,128,128]{2,1,0:T(8,128)(2,1)} %get-tuple-element.33.refs_6_), channel_id=1, source_target_pairs={{0,1},{1,2},{2,3},{3,4},{4,5},{5,6},{6,7},{7,8},{8,9},{9,10},{10,1... | collective-permute-start | bytes 3145736 | tf_op jit(solution)/shard_map/ppermute | solution.py:31
  96.9 8.6 %copy-start.2 = (f32[33,128]{1,0:T(8,128)}, f32[33,128]{1,0:T(8,128)S(1)}, u32[]{:S(2)}) copy-start(f32[33,128]{1,0:T(8,128)S(1)} %convert_reduce_fusion.first) | copy-start | bytes 50692
  96.9 4.5 %collective-permute-start.6 = (f32[33,128]{1,0:T(8,128)S(1)}, f32[33,128]{1,0:T(8,128)S(1)}, u32[]{:S(2)}, u32[]{:S(2)}) collective-permute-start(f32[33,128]{1,0:T(8,128)S(1)} %convert_reduce_fusion.first), channel_id=1, source_target_pairs={{0,96},{32,0},{64,32},{96,64},{1,97},{33,1},{65,33},{97,65},{2,98}... | collective-permute-start | bytes 50696 | tf_op jit(solution)/shard_map/ppermute | solution.py:31
  99.7 5.3 %collective-permute-start.5 = (f32[33,128]{1,0:T(8,128)S(1)}, f32[33,128]{1,0:T(8,128)S(1)}, u32[]{:S(2)}, u32[]{:S(2)}) collective-permute-start(f32[33,128]{1,0:T(8,128)S(1)} %convert_reduce_fusion.first), channel_id=1, source_target_pairs={{0,64},{32,96},{64,0},{96,32},{1,65},{33,97},{65,1},{97,33},{2,66}... | collective-permute-start | bytes 50696 | tf_op jit(solution)/shard_map/ppermute | solution.py:31
  100.5 5.0 %collective-permute-start.4 = (f32[33,128]{1,0:T(8,128)S(1)}, f32[33,128]{1,0:T(8,128)S(1)}, u32[]{:S(2)}, u32[]{:S(2)}) collective-permute-start(f32[33,128]{1,0:T(8,128)S(1)} %convert_reduce_fusion.first), channel_id=1, source_target_pairs={{0,32},{32,64},{64,96},{96,0},{1,33},{33,65},{65,97},{97,1},{2,34}... | collective-permute-start | bytes 50696 | tf_op jit(solution)/shard_map/ppermute | solution.py:31
  101.4 4.1 %copy-start.3 = (f32[33,128]{1,0:T(8,128)}, f32[33,128]{1,0:T(8,128)S(1)}, u32[]{:S(2)}) copy-start(f32[33,128]{1,0:T(8,128)S(1)} %collective-permute-done.6.fourth) | copy-start | bytes 50692
  105.0 0.6 copy-start.4
  105.6 0.6 copy-start.5

commit v4 on v3

--- a/solution.py
+++ b/solution.py
@@ -23,6 +23,7 @@
 LATER_AT = 32
 FRAME = 24
 HALVES = 1
+VMEM = 65408 * 1024
 TILES = 4
 
 
@@ -604,7 +605,7 @@
         out_specs=[pl.BlockSpec((n, cut), lambda j: (0, j)) for n in (EARLIER, LATER)],
         out_shape=[jax.ShapeDtypeStruct((n, channels), BF16) for n in (EARLIER, LATER)],
         scratch_shapes=[pltpu.VMEM((LATER_AT + LATER + 6, LANES), F32)],
-        compiler_params=pltpu.CompilerParams(vmem_limit_bytes=63 * 1024 * 1024),
+        compiler_params=pltpu.CompilerParams(vmem_limit_bytes=VMEM),
         name="rims",
     )(*[streams] * 3, res, *[streams] * 3, res, g)
     before, after = turn(before, "seq", 1), turn(after, "seq", -1)
@@ -628,7 +629,7 @@
     saved = [long, ext, ext, long, long]
     in_smem = pl.BlockSpec(memory_space=pltpu.SMEM)
     anywhere = pl.BlockSpec(memory_space=pl.ANY)
-    limit = pltpu.CompilerParams(vmem_limit_bytes=63 * 1024 * 1024)
+    limit = pltpu.CompilerParams(vmem_limit_bytes=VMEM)
     scratch = pltpu.VMEM((FRAME + ext, LANES), F32)
     row_buf = lambda n: pltpu.VMEM((n, LANES), F32)
     behind = lambda spec: moved_spec(spec, lambda j: jnp.maximum(j - 1, 0))
@@ -739,6 +740,7 @@
             jax.ShapeDtypeStruct(shape, F32)
             for shape in ((3, cols), (3, cols), (7, LANES), (GROUPS, LANES))
         ],
+        compiler_params=limit,
         name="totals",
     )(share, *others)
     return (grad_res[None], grad_streams[None], *filter_grads[:3], filter_grads[3].T)

time: 108 us -> 107 us (level)
  local copies, waits for them, and re-layouts: 2.19 us -> 0.01 us
    unnamed x12 -> x6, local copies, waits for them, and re-layouts: 2.19 us -> 0.01 us
where the time goes in v4:
time: 107 us
  Pallas kernels  51.9 us (49%)
  waiting for transfers between devices  27.2 us (25%)
  blocking collectives  13.3 us (12%)
  starting transfers between devices  12.8 us (12%)
    pallas_call x1, Pallas kernels, gradients(): pl.pallas_call(functools.partial(second_kernel, rows, channels, half), gr...  29.8 us
    ppermute x7, waiting for transfers between devices, turn(): lax.ppermute(array, axis, [(i, (i + by) % peers) for i in range(peers)])  27.2 us
    pallas_call x1, Pallas kernels, products(): pl.pallas_call(functools.partial(first_kernel, rows), grid=(half_steps,),...  14.6 us
    all_to_all x1, blocking collectives, shards(): parts = lax.all_to_all(sums, 'seq', split_axis=0, concat_axis=0, tiled=True)  13.3 us
    ppermute x7, starting transfers between devices, turn(): lax.ppermute(array, axis, [(i, (i + by) % peers) for i in range(peers)])  12.8 us
    pallas_call x1, Pallas kernels, shards(): pl.pallas_call(toeplitz_kernel, grid=(groups // LANES,), in_specs=[pl.Blo...  3.67 us
    pallas_call x1, Pallas kernels, shards(): pl.pallas_call(rim_kernel, grid=(2,), in_specs=[strip(x, last) for x in (...  2.28 us
  transfers between devices with their start and end apart: 7, of which 4 were waited for; matrix products, arithmetic and copies ran while one was open for 1% of the time, Pallas kernels for 3%

profile of v4, /device:TPU:0, one launch (start us, length us, event | category | flops | bytes accessed | tf_op | source)
XLA Modules:
  0.0 106.5 jit_solution(2608257182468740438)
XLA Ops:
  0.6 2.3 %rims.1 = (bf16[26,4096]{1,0:T(8,128)(2,1)}, bf16[50,4096]{1,0:T(8,128)(2,1)}) custom-call(bf16[128,12288]{1,0:T(8,128)(2,1)} %bitcast.8, bf16[128,12288]{1,0:T(8,128)(2,1)} %bitcast.9, bf16[128,12288]{1,0:T(8,128)(2,1)} %bitcast.10, bf16[128,4096]{1,0:T(8,128)(2,1)} %bitcast.23, bf16[128,12288]{1,0:T(8,128)(2,1)} %bitcast.11, bf16[128,12288]{1,0:T(8,128)(2,1)} %bitcast.12, ...), custom_call_target="tpu_custom_call" | custom-call | tf_op jit(solution)/shard_map/rims/pallas_call | solution.py:601
  2.9 6.1 %collective-permute-start.1 = (bf16[50,4096]{1,0:T(8,128)(2,1)}, bf16[50,4096]{1,0:T(8,128)(2,1)}, u32[]{:S(2)}, u32[]{:S(2)}) collective-permute-start(bf16[50,4096]{1,0:T(8,128)(2,1)} %get-tuple-element.29), channel_id=1, source_target_pairs={{0,31},{1,0},{2,1},{3,2},{4,3},{5,4},{6,5},{7,6},{8,7},{9,8},{10,9... | collective-permute-start | bytes 1228808 | tf_op jit(solution)/shard_map/ppermute | solution.py:32
  9.0 0.0 collective-permute-start
  9.0 3.7 %toeplitz.1 = (bf16[8192,128]{1,0:T(8,128)(2,1)}, bf16[8192,128]{1,0:T(8,128)(2,1)}) custom-call(bf16[128,256]{1,0:T(8,128)(2,1)} %taps.1), custom_call_target="tpu_custom_call" | custom-call | tf_op jit(solution)/shard_map/toeplitz/pallas_call | solution.py:615
  12.7 0.6 add_convert_fusion.refs_14_.refs_25_
  13.2 5.2 %collective-permute-done.refs_5_.refs_4_ = bf16[26,4096]{1,0:T(8,128)(2,1)} collective-permute-done((bf16[26,4096]{1,0:T(8,128)(2,1)}, bf16[26,4096]{1,0:T(8,128)(2,1)}, u32[]{:S(2)}, u32[]{:S(2)}) %collective-permute-start) | collective-permute-done | bytes 213024 | tf_op jit(solution)/shard_map/ppermute | solution.py:32
  18.4 0.0 collective-permute-done.1.refs_6_.refs_5_
  18.4 14.6 %products.1 = (bf16[32,128,128]{2,1,0:T(8,128)(2,1)}, bf16[32,16,128]{2,1,0:T(8,128)(2,1)}, bf16[32,144,128]{2,1,0:T(8,128)(2,1)}, bf16[32,160,128]{2,1,0:T(8,12...) custom-call(bf16[128,12288]{1,0:T(8,128)(2,1)} %bitcast.14, ...), custom_call_target="tpu_custom_call" | custom-call | tf_op jit(solution)/shard_map/products/pallas_call | solution.py:649
  33.0 2.2 %collective-permute-start.3 = (bf16[32,144,128]{2,1,0:T(8,128)(2,1)}, bf16[32,144,128]{2,1,0:T(8,128)(2,1)}, u32[]{:S(2)}, u32[]{:S(2)}) collective-permute-start(bf16[32,144,128]{2,1,0:T(8,128)(2,1)} %get-tuple-element.35.refs_9_), channel_id=1, source_target_pairs={{0,31},{1,0},{2,1},{3,2},{4,3},{5,4},{6,5},{7,6},{8,7},{9,8},{10,9... | collective-permute-start | bytes 3538952 | tf_op jit(solution)/shard_map/ppermute | solution.py:32
  35.1 0.0 collective-permute-start.2
  35.2 17.9 %collective-permute-done.2.refs_8_ = bf16[32,128,128]{2,1,0:T(8,128)(2,1)} collective-permute-done((bf16[32,128,128]{2,1,0:T(8,128)(2,1)}, bf16[32,128,128]{2,1,0:T(8,128)(2,1)}, u32[]{:S(2)}, u32[]{:S(2)}) %collective-permute-start.2) | collective-permute-done | bytes 1048608 | tf_op jit(solution)/shard_map/ppermute | solution.py:32
  53.0 0.0 collective-permute-done.3.refs_10_
  53.0 29.8 %gradients.1 = (bf16[128,4096]{1,0:T(8,128)(2,1)}, bf16[128,12288]{1,0:T(8,128)(2,1)}, bf16[32,33,128]{2,1,0:T(8,128)(2,1)}) custom-call(bf16[128,12288]{1,0:T(8,128)(2,1)} %bitcast.17, bf16[128,12288]{1,0:T(8,128)(2,1)} %bitcast.18, bf16[128,12288]{1,0:T(8,128)(2,1)} %bitcast.19, bf16[128,4096]{1,0:T(8,128)(2,1)} %bitcast.22, ...), custom_call_target="tpu_custom_call" | custom-call | tf_op jit(solution)/shard_map/gradients/pallas_call | solution.py:679
  82.8 13.3 %all_to_all.5 = bf16[32,33,128]{2,1,0:T(8,128)(2,1)S(1)} all-to-all(bf16[32,33,128]{2,1,0:T(8,128)(2,1)} %get-tuple-element.45), channel_id=1, replica_groups=mesh['dp'=4,'seq'=32] {'seq'}, dimensions={0} | all-to-all | bytes 540672 | tf_op jit(solution)/shard_map/all_to_all | solution.py:733
  96.1 0.1 convert_reduce_fusion.first
  96.2 0.0 copy-start
  96.2 2.8 %collective-permute-start.6 = (f32[33,128]{1,0:T(8,128)S(1)}, f32[33,128]{1,0:T(8,128)S(1)}, u32[]{:S(2)}, u32[]{:S(2)}) collective-permute-start(f32[33,128]{1,0:T(8,128)S(1)} %convert_reduce_fusion.first), channel_id=1, source_target_pairs={{0,96},{32,0},{64,32},{96,64},{1,97},{33,1},{65,33},{97,65},{2,98}... | collective-permute-start | bytes 50696 | tf_op jit(solution)/shard_map/ppermute | solution.py:32
  99.0 0.8 collective-permute-start.5
  99.8 0.9 collective-permute-start.4
  100.7 0.0 collective-permute-done.6.fourth
  100.7 0.0 copy-start.1
  100.7 3.6 %collective-permute-done.5.third = f32[33,128]{1,0:T(8,128)S(1)} collective-permute-done((f32[33,128]{1,0:T(8,128)S(1)}, f32[33,128]{1,0:T(8,128)S(1)}, u32[]{:S(2)}, u32[]{:S(2)}) %collective-permute-start.5) | collective-permute-done | bytes 16928 | tf_op jit(solution)/shard_map/ppermute | solution.py:32
  104.3 0.0 copy-start.2
  104.3 0.6 collective-permute-done.4.second
  104.9 0.0 copy-done
  104.9 0.0 copy-done.1
  104.9 0.0 copy-done.2
  104.9 1.6 %totals.1 = (f32[3,384]{1,0:T(4,128)}, f32[3,384]{1,0:T(4,128)}, f32[7,128]{1,0:T(8,128)}, f32[8,128]{1,0:T(8,128)}) custom-call(f32[33,128]{1,0:T(8,128)} %copy-done, f32[33,128]{1,0:T(8,128)} %collective-permute-done.4.second, f32[33,128]{1,0:T(8,128)} %copy-done.2, f32[33,128]{1,0:T(8,128)} %copy-done.1), custom_call_target="tpu_custom_call" | custom-call | tf_op jit(solution)/shard_map/totals/pallas_call | solution.py:737
Async XLA Ops:
  2.9 15.5 %collective-permute-start.1 = (bf16[50,4096]{1,0:T(8,128)(2,1)}, bf16[50,4096]{1,0:T(8,128)(2,1)}, u32[]{:S(2)}, u32[]{:S(2)}) collective-permute-start(bf16[50,4096]{1,0:T(8,128)(2,1)} %get-tuple-element.29), channel_id=1, source_target_pairs={{0,31},{1,0},{2,1},{3,2},{4,3},{5,4},{6,5},{7,6},{8,7},{9,8},{10,9... | collective-permute-start | bytes 1228808 | tf_op jit(solution)/shard_map/ppermute | solution.py:32
  9.0 9.4 %collective-permute-start = (bf16[26,4096]{1,0:T(8,128)(2,1)}, bf16[26,4096]{1,0:T(8,128)(2,1)}, u32[]{:S(2)}, u32[]{:S(2)}) collective-permute-start(bf16[26,4096]{1,0:T(8,128)(2,1)} %get-tuple-element.28), channel_id=1, source_target_pairs={{0,1},{1,2},{2,3},{3,4},{4,5},{5,6},{6,7},{7,8},{8,9},{9,10},{10,1... | collective-permute-start | bytes 638984 | tf_op jit(solution)/shard_map/ppermute | solution.py:32
  33.0 20.0 %collective-permute-start.3 = (bf16[32,144,128]{2,1,0:T(8,128)(2,1)}, bf16[32,144,128]{2,1,0:T(8,128)(2,1)}, u32[]{:S(2)}, u32[]{:S(2)}) collective-permute-start(bf16[32,144,128]{2,1,0:T(8,128)(2,1)} %get-tuple-element.35.refs_9_), channel_id=1, source_target_pairs={{0,31},{1,0},{2,1},{3,2},{4,3},{5,4},{6,5},{7,6},{8,7},{9,8},{10,9... | collective-permute-start | bytes 3538952 | tf_op jit(solution)/shard_map/ppermute | solution.py:32
  35.1 17.9 %collective-permute-start.2 = (bf16[32,128,128]{2,1,0:T(8,128)(2,1)}, bf16[32,128,128]{2,1,0:T(8,128)(2,1)}, u32[]{:S(2)}, u32[]{:S(2)}) collective-permute-start(bf16[32,128,128]{2,1,0:T(8,128)(2,1)} %get-tuple-element.33.refs_6_), channel_id=1, source_target_pairs={{0,1},{1,2},{2,3},{3,4},{4,5},{5,6},{6,7},{7,8},{8,9},{9,10},{10,1... | collective-permute-start | bytes 3145736 | tf_op jit(solution)/shard_map/ppermute | solution.py:32
  96.2 8.7 %copy-start = (f32[33,128]{1,0:T(8,128)}, f32[33,128]{1,0:T(8,128)S(1)}, u32[]{:S(2)}) copy-start(f32[33,128]{1,0:T(8,128)S(1)} %convert_reduce_fusion.first) | copy-start | bytes 50692
  96.2 4.5 %collective-permute-start.6 = (f32[33,128]{1,0:T(8,128)S(1)}, f32[33,128]{1,0:T(8,128)S(1)}, u32[]{:S(2)}, u32[]{:S(2)}) collective-permute-start(f32[33,128]{1,0:T(8,128)S(1)} %convert_reduce_fusion.first), channel_id=1, source_target_pairs={{0,96},{32,0},{64,32},{96,64},{1,97},{33,1},{65,33},{97,65},{2,98}... | collective-permute-start | bytes 50696 | tf_op jit(solution)/shard_map/ppermute | solution.py:32
  99.0 5.3 %collective-permute-start.5 = (f32[33,128]{1,0:T(8,128)S(1)}, f32[33,128]{1,0:T(8,128)S(1)}, u32[]{:S(2)}, u32[]{:S(2)}) collective-permute-start(f32[33,128]{1,0:T(8,128)S(1)} %convert_reduce_fusion.first), channel_id=1, source_target_pairs={{0,64},{32,96},{64,0},{96,32},{1,65},{33,97},{65,1},{97,33},{2,66}... | collective-permute-start | bytes 50696 | tf_op jit(solution)/shard_map/ppermute | solution.py:32
  99.8 5.1 %collective-permute-start.4 = (f32[33,128]{1,0:T(8,128)S(1)}, f32[33,128]{1,0:T(8,128)}, u32[]{:S(2)}, u32[]{:S(2)}) collective-permute-start(f32[33,128]{1,0:T(8,128)S(1)} %convert_reduce_fusion.first), channel_id=1, source_target_pairs={{0,32},{32,64},{64,96},{96,0},{1,33},{33,65},{65,97},{97,1},{2,34}... | collective-permute-start | bytes 50696 | tf_op jit(solution)/shard_map/ppermute | solution.py:32
  100.7 4.2 %copy-start.1 = (f32[33,128]{1,0:T(8,128)}, f32[33,128]{1,0:T(8,128)S(1)}, u32[]{:S(2)}) copy-start(f32[33,128]{1,0:T(8,128)S(1)} %collective-permute-done.6.fourth) | copy-start | bytes 50692
  104.3 0.6 copy-start.2

commit v5 on v4

--- a/solution.py
+++ b/solution.py
@@ -146,7 +146,7 @@
         d_own[i, rows : rows + GROUP, :] = slopes[GROUPS]
         return carry
 
-    lax.fori_loop(0, TILES, one_tile, 0)
+    lax.fori_loop(0, TILES, one_tile, 0, unroll=True)
 
 
 def windows(low, high, last, block):

time: 107 us -> 104 us (0.972)
  Pallas kernels: 51.9 us -> 49 us
    pallas_call x1, Pallas kernels: 14.6 us -> 11.7 us  [products(): pl.pallas_call(functools.partial(first_kernel, rows), grid=(half_steps,),...]
  transfers between devices with their start and end apart: 7 -> 7, of which waited for: 4 -> 4; matrix products, arithmetic and copies ran while one was open for 1% -> 1% of each run, Pallas kernels for 3% -> 4%
where the time goes in v5:
time: 104 us
  Pallas kernels  49 us (47%)
  waiting for transfers between devices  27.2 us (26%)
  blocking collectives  13.3 us (13%)
  starting transfers between devices  12.8 us (12%)
    pallas_call x1, Pallas kernels, gradients(): pl.pallas_call(functools.partial(second_kernel, rows, channels, half), gr...  29.8 us
    ppermute x7, waiting for transfers between devices, turn(): lax.ppermute(array, axis, [(i, (i + by) % peers) for i in range(peers)])  27.2 us
    all_to_all x1, blocking collectives, shards(): parts = lax.all_to_all(sums, 'seq', split_axis=0, concat_axis=0, tiled=True)  13.3 us
    ppermute x7, starting transfers between devices, turn(): lax.ppermute(array, axis, [(i, (i + by) % peers) for i in range(peers)])  12.8 us
    pallas_call x1, Pallas kernels, products(): pl.pallas_call(functools.partial(first_kernel, rows), grid=(half_steps,),...  11.7 us
    pallas_call x1, Pallas kernels, shards(): pl.pallas_call(toeplitz_kernel, grid=(groups // LANES,), in_specs=[pl.Blo...  3.67 us
    pallas_call x1, Pallas kernels, shards(): pl.pallas_call(rim_kernel, grid=(2,), in_specs=[strip(x, last) for x in (...  2.28 us
  transfers between devices with their start and end apart: 7, of which 4 were waited for; matrix products, arithmetic and copies ran while one was open for 1% of the time, Pallas kernels for 4%

profile of v5, /device:TPU:0, one launch (start us, length us, event | category | flops | bytes accessed | tf_op | source)
XLA Modules:
  0.0 103.7 jit_solution(12441256713410635518)
XLA Ops:
  0.6 2.3 %rims.1 = (bf16[26,4096]{1,0:T(8,128)(2,1)}, bf16[50,4096]{1,0:T(8,128)(2,1)}) custom-call(bf16[128,12288]{1,0:T(8,128)(2,1)} %bitcast.8, bf16[128,12288]{1,0:T(8,128)(2,1)} %bitcast.9, bf16[128,12288]{1,0:T(8,128)(2,1)} %bitcast.10, bf16[128,4096]{1,0:T(8,128)(2,1)} %bitcast.23, bf16[128,12288]{1,0:T(8,128)(2,1)} %bitcast.11, bf16[128,12288]{1,0:T(8,128)(2,1)} %bitcast.12, ...), custom_call_target="tpu_custom_call" | custom-call | tf_op jit(solution)/shard_map/rims/pallas_call | solution.py:601
  2.9 6.1 %collective-permute-start.1 = (bf16[50,4096]{1,0:T(8,128)(2,1)}, bf16[50,4096]{1,0:T(8,128)(2,1)}, u32[]{:S(2)}, u32[]{:S(2)}) collective-permute-start(bf16[50,4096]{1,0:T(8,128)(2,1)} %get-tuple-element.29), channel_id=1, source_target_pairs={{0,31},{1,0},{2,1},{3,2},{4,3},{5,4},{6,5},{7,6},{8,7},{9,8},{10,9... | collective-permute-start | bytes 1228808 | tf_op jit(solution)/shard_map/ppermute | solution.py:32
  9.0 0.0 collective-permute-start
  9.0 3.7 %toeplitz.1 = (bf16[8192,128]{1,0:T(8,128)(2,1)}, bf16[8192,128]{1,0:T(8,128)(2,1)}) custom-call(bf16[128,256]{1,0:T(8,128)(2,1)} %taps.1), custom_call_target="tpu_custom_call" | custom-call | tf_op jit(solution)/shard_map/toeplitz/pallas_call | solution.py:615
  12.7 0.6 add_convert_fusion.refs_14_.refs_25_
  13.2 5.2 %collective-permute-done.refs_5_.refs_4_ = bf16[26,4096]{1,0:T(8,128)(2,1)} collective-permute-done((bf16[26,4096]{1,0:T(8,128)(2,1)}, bf16[26,4096]{1,0:T(8,128)(2,1)}, u32[]{:S(2)}, u32[]{:S(2)}) %collective-permute-start) | collective-permute-done | bytes 213024 | tf_op jit(solution)/shard_map/ppermute | solution.py:32
  18.4 0.0 collective-permute-done.1.refs_6_.refs_5_
  18.4 11.7 %products.1 = (bf16[32,128,128]{2,1,0:T(8,128)(2,1)}, bf16[32,16,128]{2,1,0:T(8,128)(2,1)}, bf16[32,144,128]{2,1,0:T(8,128)(2,1)}, bf16[32,160,128]{2,1,0:T(8,12...) custom-call(bf16[128,12288]{1,0:T(8,128)(2,1)} %bitcast.14, ...), custom_call_target="tpu_custom_call" | custom-call | tf_op jit(solution)/shard_map/products/pallas_call | solution.py:649
  30.1 2.2 %collective-permute-start.3 = (bf16[32,144,128]{2,1,0:T(8,128)(2,1)}, bf16[32,144,128]{2,1,0:T(8,128)(2,1)}, u32[]{:S(2)}, u32[]{:S(2)}) collective-permute-start(bf16[32,144,128]{2,1,0:T(8,128)(2,1)} %get-tuple-element.35.refs_9_), channel_id=1, source_target_pairs={{0,31},{1,0},{2,1},{3,2},{4,3},{5,4},{6,5},{7,6},{8,7},{9,8},{10,9... | collective-permute-start | bytes 3538952 | tf_op jit(solution)/shard_map/ppermute | solution.py:32
  32.3 0.0 collective-permute-start.2
  32.3 17.9 %collective-permute-done.2.refs_8_ = bf16[32,128,128]{2,1,0:T(8,128)(2,1)} collective-permute-done((bf16[32,128,128]{2,1,0:T(8,128)(2,1)}, bf16[32,128,128]{2,1,0:T(8,128)(2,1)}, u32[]{:S(2)}, u32[]{:S(2)}) %collective-permute-start.2) | collective-permute-done | bytes 1048608 | tf_op jit(solution)/shard_map/ppermute | solution.py:32
  50.1 0.0 collective-permute-done.3.refs_10_
  50.1 29.8 %gradients.1 = (bf16[128,4096]{1,0:T(8,128)(2,1)}, bf16[128,12288]{1,0:T(8,128)(2,1)}, bf16[32,33,128]{2,1,0:T(8,128)(2,1)}) custom-call(bf16[128,12288]{1,0:T(8,128)(2,1)} %bitcast.17, bf16[128,12288]{1,0:T(8,128)(2,1)} %bitcast.18, bf16[128,12288]{1,0:T(8,128)(2,1)} %bitcast.19, bf16[128,4096]{1,0:T(8,128)(2,1)} %bitcast.22, ...), custom_call_target="tpu_custom_call" | custom-call | tf_op jit(solution)/shard_map/gradients/pallas_call | solution.py:679
  80.0 13.3 %all_to_all.5 = bf16[32,33,128]{2,1,0:T(8,128)(2,1)S(1)} all-to-all(bf16[32,33,128]{2,1,0:T(8,128)(2,1)} %get-tuple-element.45), channel_id=1, replica_groups=mesh['dp'=4,'seq'=32] {'seq'}, dimensions={0} | all-to-all | bytes 540672 | tf_op jit(solution)/shard_map/all_to_all | solution.py:733
  93.2 0.1 convert_reduce_fusion.first
  93.3 0.0 copy-start
  93.3 2.8 %collective-permute-start.6 = (f32[33,128]{1,0:T(8,128)S(1)}, f32[33,128]{1,0:T(8,128)S(1)}, u32[]{:S(2)}, u32[]{:S(2)}) collective-permute-start(f32[33,128]{1,0:T(8,128)S(1)} %convert_reduce_fusion.first), channel_id=1, source_target_pairs={{0,96},{32,0},{64,32},{96,64},{1,97},{33,1},{65,33},{97,65},{2,98}... | collective-permute-start | bytes 50696 | tf_op jit(solution)/shard_map/ppermute | solution.py:32
  96.1 0.8 collective-permute-start.5
  96.9 0.9 collective-permute-start.4
  97.8 0.0 collective-permute-done.6.fourth
  97.8 0.0 copy-start.1
  97.8 3.6 %collective-permute-done.5.third = f32[33,128]{1,0:T(8,128)S(1)} collective-permute-done((f32[33,128]{1,0:T(8,128)S(1)}, f32[33,128]{1,0:T(8,128)S(1)}, u32[]{:S(2)}, u32[]{:S(2)}) %collective-permute-start.5) | collective-permute-done | bytes 16928 | tf_op jit(solution)/shard_map/ppermute | solution.py:32
  101.4 0.0 copy-start.2
  101.4 0.6 collective-permute-done.4.second
  102.0 0.0 copy-done
  102.0 0.0 copy-done.1
  102.0 0.0 copy-done.2
  102.1 1.6 %totals.1 = (f32[3,384]{1,0:T(4,128)}, f32[3,384]{1,0:T(4,128)}, f32[7,128]{1,0:T(8,128)}, f32[8,128]{1,0:T(8,128)}) custom-call(f32[33,128]{1,0:T(8,128)} %copy-done, f32[33,128]{1,0:T(8,128)} %collective-permute-done.4.second, f32[33,128]{1,0:T(8,128)} %copy-done.2, f32[33,128]{1,0:T(8,128)} %copy-done.1), custom_call_target="tpu_custom_call" | custom-call | tf_op jit(solution)/shard_map/totals/pallas_call | solution.py:737
Async XLA Ops:
  2.9 15.5 %collective-permute-start.1 = (bf16[50,4096]{1,0:T(8,128)(2,1)}, bf16[50,4096]{1,0:T(8,128)(2,1)}, u32[]{:S(2)}, u32[]{:S(2)}) collective-permute-start(bf16[50,4096]{1,0:T(8,128)(2,1)} %get-tuple-element.29), channel_id=1, source_target_pairs={{0,31},{1,0},{2,1},{3,2},{4,3},{5,4},{6,5},{7,6},{8,7},{9,8},{10,9... | collective-permute-start | bytes 1228808 | tf_op jit(solution)/shard_map/ppermute | solution.py:32
  9.0 9.4 %collective-permute-start = (bf16[26,4096]{1,0:T(8,128)(2,1)}, bf16[26,4096]{1,0:T(8,128)(2,1)}, u32[]{:S(2)}, u32[]{:S(2)}) collective-permute-start(bf16[26,4096]{1,0:T(8,128)(2,1)} %get-tuple-element.28), channel_id=1, source_target_pairs={{0,1},{1,2},{2,3},{3,4},{4,5},{5,6},{6,7},{7,8},{8,9},{9,10},{10,1... | collective-permute-start | bytes 638984 | tf_op jit(solution)/shard_map/ppermute | solution.py:32
  30.1 20.0 %collective-permute-start.3 = (bf16[32,144,128]{2,1,0:T(8,128)(2,1)}, bf16[32,144,128]{2,1,0:T(8,128)(2,1)}, u32[]{:S(2)}, u32[]{:S(2)}) collective-permute-start(bf16[32,144,128]{2,1,0:T(8,128)(2,1)} %get-tuple-element.35.refs_9_), channel_id=1, source_target_pairs={{0,31},{1,0},{2,1},{3,2},{4,3},{5,4},{6,5},{7,6},{8,7},{9,8},{10,9... | collective-permute-start | bytes 3538952 | tf_op jit(solution)/shard_map/ppermute | solution.py:32
  32.3 17.9 %collective-permute-start.2 = (bf16[32,128,128]{2,1,0:T(8,128)(2,1)}, bf16[32,128,128]{2,1,0:T(8,128)(2,1)}, u32[]{:S(2)}, u32[]{:S(2)}) collective-permute-start(bf16[32,128,128]{2,1,0:T(8,128)(2,1)} %get-tuple-element.33.refs_6_), channel_id=1, source_target_pairs={{0,1},{1,2},{2,3},{3,4},{4,5},{5,6},{6,7},{7,8},{8,9},{9,10},{10,1... | collective-permute-start | bytes 3145736 | tf_op jit(solution)/shard_map/ppermute | solution.py:32
  93.3 8.7 %copy-start = (f32[33,128]{1,0:T(8,128)}, f32[33,128]{1,0:T(8,128)S(1)}, u32[]{:S(2)}) copy-start(f32[33,128]{1,0:T(8,128)S(1)} %convert_reduce_fusion.first) | copy-start | bytes 50692
  93.3 4.5 %collective-permute-start.6 = (f32[33,128]{1,0:T(8,128)S(1)}, f32[33,128]{1,0:T(8,128)S(1)}, u32[]{:S(2)}, u32[]{:S(2)}) collective-permute-start(f32[33,128]{1,0:T(8,128)S(1)} %convert_reduce_fusion.first), channel_id=1, source_target_pairs={{0,96},{32,0},{64,32},{96,64},{1,97},{33,1},{65,33},{97,65},{2,98}... | collective-permute-start | bytes 50696 | tf_op jit(solution)/shard_map/ppermute | solution.py:32
  96.1 5.3 %collective-permute-start.5 = (f32[33,128]{1,0:T(8,128)S(1)}, f32[33,128]{1,0:T(8,128)S(1)}, u32[]{:S(2)}, u32[]{:S(2)}) collective-permute-start(f32[33,128]{1,0:T(8,128)S(1)} %convert_reduce_fusion.first), channel_id=1, source_target_pairs={{0,64},{32,96},{64,0},{96,32},{1,65},{33,97},{65,1},{97,33},{2,66}... | collective-permute-start | bytes 50696 | tf_op jit(solution)/shard_map/ppermute | solution.py:32
  96.9 5.1 %collective-permute-start.4 = (f32[33,128]{1,0:T(8,128)S(1)}, f32[33,128]{1,0:T(8,128)}, u32[]{:S(2)}, u32[]{:S(2)}) collective-permute-start(f32[33,128]{1,0:T(8,128)S(1)} %convert_reduce_fusion.first), channel_id=1, source_target_pairs={{0,32},{32,64},{64,96},{96,0},{1,33},{33,65},{65,97},{97,1},{2,34}... | collective-permute-start | bytes 50696 | tf_op jit(solution)/shard_map/ppermute | solution.py:32
  97.8 4.2 %copy-start.1 = (f32[33,128]{1,0:T(8,128)}, f32[33,128]{1,0:T(8,128)S(1)}, u32[]{:S(2)}) copy-start(f32[33,128]{1,0:T(8,128)S(1)} %collective-permute-done.6.fourth) | copy-start | bytes 50692
  101.4 0.6 copy-start.2
